TPU v7x, 32 devices: a whole 2x2x4 slice. The times are simulated.
32 devices in a mesh: samp: 2 (over x), feat: 16 (over z, y, core).
Axes of the slice: x: 2, y: 2, z: 4, core: 2. Of those that a mesh axis runs over, the one named last changes fastest.
Arguments:
- embeddings: bfloat16 [2048, 1024], P('samp'), may hold values from -6 to 6
- frequencies: bfloat16 [1024, 8192], P(None, 'feat'), may hold values from -0.1875 to 0.1875
- phases: float32 [8192], P('feat'), may hold values from -3.140625 to 3.140625
- treat_freq: float32 [8192], P('feat'), may hold values from -3.140625 to 3.140625
- treatment: int32 [2048], P('samp'), may hold values from 0 to 1
- flips: int32 [2048], P('samp'), may hold values from 0 to 1
- panel: int32 [1], replicated, may hold values from 0 to 15
Outputs:
- schur: float32 [8192, 8192], P('samp', 'feat')
- panel_factor: float32 [8192, 512], P('samp')
- moment_scaled: float32 [8192], P('feat')
All inputs are finite; a program needn't handle non-finite values.
Results may differ from a plain program's by a relative error of at most 0.0032.
Values may be sent and summed in bfloat16 or wider, within the bound.
A program may use at most 128 MiB of HBM per device.

v0:
```python
import jax
import jax.numpy as jnp
from jax import lax
from jax.sharding import PartitionSpec as P

PANEL = 512


ridge = 0.1
root_two = 1.4142135623730951


def broadcast(shard, axis, root):
    mine = lax.axis_index(axis) == root
    return lax.psum(jnp.where(mine, shard, jnp.zeros_like(shard)), axis)


def cosine_map(project, phases, treat_freq, treated):
    return root_two * jnp.cos(project + phases[None, :] + treated[:, None] * treat_freq[None, :])


def inner_rows(left, right):
    return lax.dot_general(
        left, right, (((0,), (0,)), ((), ())), preferred_element_type=jnp.float32
    )


def per_device(embeddings, frequencies, phases, treat_freq, treatment, flips, panel):
    project = jnp.dot(embeddings, frequencies, preferred_element_type=jnp.float32)
    treated = treatment.astype(jnp.float32)
    flipped = flips.astype(jnp.float32)
    counter = treated + flipped - 2.0 * treated * flipped
    observed = cosine_map(project, phases, treat_freq, treated)
    counterfactual = cosine_map(project, phases, treat_freq, counter)
    feature_obs = observed.astype(jnp.bfloat16)
    samp_size = lax.axis_size("samp")
    feat_size = lax.axis_size("feat")
    sample_count = embeddings.shape[0] * samp_size
    col_width = feature_obs.shape[1]
    feat_total = col_width * feat_size
    row_height = feat_total // samp_size
    samp_index = lax.axis_index("samp")
    feat_index = lax.axis_index("feat")
    moment_part = jnp.sum(counterfactual - observed, axis=0)
    moment_sum = lax.psum(moment_part, "samp") / sample_count
    first_col = panel[0] * PANEL
    panel_devs = PANEL // col_width
    first_dev = first_col // col_width
    gram_part = inner_rows(lax.all_gather(feature_obs, "feat", axis=1, tiled=True), feature_obs)
    gram_raw = lax.psum_scatter(gram_part, "samp", scatter_dimension=0, tiled=True)
    row_ids = samp_index * row_height + lax.broadcasted_iota(jnp.int32, (row_height, col_width), 0)
    col_ids = feat_index * col_width + lax.broadcasted_iota(jnp.int32, (row_height, col_width), 1)
    gram_own = gram_raw / sample_count + ridge * (row_ids == col_ids).astype(jnp.float32)
    col_parts = []
    moment_parts = []
    for member in range(panel_devs):
        got_cols, got_moment = (
            broadcast(gram_own, "feat", first_dev + member),
            broadcast(moment_sum, "feat", first_dev + member),
        )
        col_parts.append(got_cols)
        moment_parts.append(got_moment)
    panel_cols = jnp.concatenate(col_parts, axis=1)
    moment_panel = jnp.concatenate(moment_parts, axis=0)
    source_samp = first_col // row_height
    offset_row = first_col % row_height
    pivot_local = lax.dynamic_slice_in_dim(panel_cols, offset_row, PANEL, 0)
    cross_local = lax.dynamic_slice_in_dim(gram_own, offset_row, PANEL, 0)
    pivot, cross = (
        broadcast(pivot_local, "samp", source_samp),
        broadcast(cross_local, "samp", source_samp),
    )
    lower = jnp.linalg.cholesky(pivot)
    factor_t = lax.linalg.triangular_solve(lower, panel_cols.T, left_side=True, lower=True)
    panel_factor = factor_t.T
    cross_t = lax.linalg.triangular_solve(lower, cross, left_side=True, lower=True)
    schur = gram_own - jnp.dot(panel_factor, cross_t, precision=lax.Precision.HIGHEST)
    solved = lax.linalg.triangular_solve(lower, moment_panel[:, None], left_side=True, lower=True)[
        :, 0
    ]
    reduced = moment_sum - jnp.dot(cross_t.T, solved, precision=lax.Precision.HIGHEST)
    moment_scaled = jnp.sqrt(jnp.float32(sample_count)) * reduced
    return (schur, panel_factor, moment_scaled)


def solution(mesh):
    return jax.shard_map(
        per_device,
        mesh=mesh,
        in_specs=(
            P("samp", None),
            P(None, "feat"),
            P("feat"),
            P("feat"),
            P("samp"),
            P("samp"),
            P(),
        ),
        out_specs=(P("samp", "feat"), P("samp", None), P("feat")),
        check_vma=False,
    )
```

profile of v0, /device:TPU:0, one launch (start us, length us, event | category | flops | bytes accessed | tf_op | source)
XLA Modules:
  0.0 819.6 jit_solution(15838278446025267421)
XLA Ops:
  8.8 17.5 %subtract_reduce_fusion = (f32[512]{0:T(512)S(1)}, bf16[1024,512]{1,0:T(8,128)(2,1)}) fusion(f32[1024]{0:T(1024)S(1)} %multiply_subtract_fusion, f32[512]{0:T(512)} %param.10, f32[1024]{0:T(1024)S(1)} %convert_element_type.10, f32[512]{0:T(512)} %param.9, bf16[1024,1024]{1,0:T(8,128)(2,1)S(1)} %copy-done, bf16[1024,512]{1,0:T(8,128)(2,1)} %param.8), kind=kOutput, calls=%fused_computation.21 | convolution fusion | flops 1078984192 | bytes 4208640 | tf_op jit(solution)/shard_map/dot_general | solution.py:29
  26.3 133.2 %all-gather.2.cloned.1.call-done = bf16[1024,8192]{1,0:T(8,128)(2,1)} async-done(((bf16[1024,512]{1,0:T(8,128)(2,1)}), bf16[1024,8192]{1,0:T(8,128)(2,1)}) %all-gather.2.cloned.1.call-update) | async-done | bytes 16777232 | tf_op jit(solution)/shard_map/all_gather | solution.py:49
  159.5 16.0 %fusion.87 = f32[8192,512]{0,1:T(8,128)} fusion(bf16[1024,8192]{1,0:T(8,128)(2,1)} %all-gather.2.cloned.1.call-done, bf16[1024,512]{1,0:T(8,128)(2,1)} %get-tuple-element.33), kind=kOutput, calls=%fused_computation.143 | convolution fusion | flops 8589934592 | bytes 34603008 | tf_op jit(solution)/shard_map/dot_general | solution.py:23
  176.3 186.7 %reduce-scatter.2.cloned.1.call-done = f32[4096,512]{0,1:T(8,128)} async-done(((f32[8192,512]{0,1:T(8,128)}), f32[4096,512]{0,1:T(8,128)}) %reduce-scatter.2.cloned.1.call-update) | async-done | bytes 8388624 | tf_op jit(solution)/shard_map/reduce_scatter | solution.py:50
  363.0 9.5 %broadcast_select_fusion = (f32[4096,512]{0,1:T(8,128)}, f32[4096,512]{0,1:T(8,128)}) fusion(pred[]{:T(512)S(6)} %eq.15, s32[512]{0:T(512)S(1)} %iota_add_fusion.1, s32[4096]{0:T(1024)S(1)} %iota_add_fusion, f32[4096,512]{0,1:T(8,128)} %reduce-scatter.2.cloned.1.call-done), kind=kLoop, calls=%fused_computation.18 | loop fusion | flops 10485760 | bytes 25184256 | tf_op jit(solution)/shard_map/jit(_where)/select_n | solution.py:15
  372.6 2.6 dynamic-slice_select_fusion
  375.2 167.3 %all-reduce.5.cloned.1.call-done = f32[4096,512]{0,1:T(8,128)} async-done(((f32[4096,512]{0,1:T(8,128)}), f32[4096,512]{0,1:T(8,128)}) %all-reduce.5.cloned.1.call-update) | async-done | bytes 8388624 | tf_op jit(solution)/shard_map/psum | solution.py:15
  542.6 2.6 dynamic-slice_select_fusion.1
  545.2 4.9 psum.38
  550.2 31.2 %psum.39 = f32[512]{0:T(512)S(1)} all-reduce(f32[512]{0:T(512)S(1)} %multiply_select_fusion), channel_id=1, replica_groups=mesh['samp'=2,'feat'=16] {'feat'}, use_global_device_ids=true, to_apply=%region_14.15 | all-reduce | flops 512 | bytes 4096 | tf_op jit(solution)/shard_map/psum | solution.py:15
  581.4 26.9 %all-reduce.7.cloned.1.call-done = (f32[512,512]{0,1:T(8,128)}, f32[512,512]{0,1:T(8,128)}) async-done(((f32[512,512]{0,1:T(8,128)}, f32[512,512]{0,1:T(8,128)}), (f32[512,512]{0,1:T(8,128)}, f32[512,512]{0,1:T(8,128)})) %all-reduce.7.cloned.1.call-update) | async-done | bytes 2097168 | tf_op jit(solution)/shard_map/psum | solution.py:15
  608.3 1.6 copy.11
  610.2 11.7 %cholesky.103 = f32[128,128]{1,0:T(8,128)S(1)} custom-call(f32[128,128]{1,0:T(8,128)S(1)} %cholesky.263), custom_call_target="Cholesky" | custom-call | tf_op jit(solution)/shard_map/jit(cholesky)/cholesky | solution.py:73
  622.0 9.8 %custom-call.34 = f32[1,128,128]{1,2,0:T(8,128)S(1)} custom-call(f32[1,128,128]{2,1,0:T(8,128)S(1)} %get-tuple-element.39), custom_call_target="InvertDiagBlocksLowerTriangular" | custom-call | tf_op jit(solution)/shard_map/jit(cholesky)/cholesky | solution.py:73
  632.5 11.7 %cholesky.215 = f32[128,128]{1,0:T(8,128)S(1)} custom-call(f32[128,128]{1,0:T(8,128)S(1)} %cholesky.267), custom_call_target="Cholesky" | custom-call | tf_op jit(solution)/shard_map/jit(cholesky)/cholesky | solution.py:73
  644.6 10.3 %custom-call.35 = f32[1,128,128]{1,2,0:T(8,128)S(1)} custom-call(f32[1,128,128]{2,1,0:T(8,128)S(1)} %get-tuple-element.37), custom_call_target="InvertDiagBlocksLowerTriangular" | custom-call | tf_op jit(solution)/shard_map/jit(cholesky)/cholesky | solution.py:73
  655.9 11.7 %cholesky.236 = f32[128,128]{1,0:T(8,128)S(1)} custom-call(f32[128,128]{1,0:T(8,128)S(1)} %cholesky.272), custom_call_target="Cholesky" | custom-call | tf_op jit(solution)/shard_map/jit(cholesky)/cholesky | solution.py:73
  667.8 9.8 %custom-call.36 = f32[1,128,128]{1,2,0:T(8,128)S(1)} custom-call(f32[1,128,128]{2,1,0:T(8,128)S(1)} %get-tuple-element.35), custom_call_target="InvertDiagBlocksLowerTriangular" | custom-call | tf_op jit(solution)/shard_map/jit(cholesky)/cholesky | solution.py:73
  678.4 11.9 %cholesky.253 = f32[128,128]{1,0:T(8,128)S(1)} custom-call(f32[128,128]{1,0:T(8,128)S(1)} %convolution_subtract_fusion.8), custom_call_target="Cholesky" | custom-call | tf_op jit(solution)/shard_map/jit(cholesky)/cholesky | solution.py:73
  695.2 10.8 %while.1 = (s32[]{:T(128)}, f32[512,512]{0,1:T(8,128)S(1)}, s32[4,2]{0,1:T(2,128)S(1)}, f32[4,128,128]{2,1,0:T(8,128)}, s32[]{:T(128)}) while((s32[]{:T(128)}, f32[512,512]{0,1:T(8,128)S(1)}, s32[4,2]{0,1:T(2,128)S(1)}, f32[4,128,128]{2,1,0:T(8,128)}, s32[]{:T(128)}) %tuple.31), condition=%wide.while_cond, body=%wide.while_body.sunk | while | flops 2 | bytes 393829 | solution.py:74
  706.0 40.1 %custom-call.37 = f32[4,128,128]{1,2,0:T(8,128)S(1)} custom-call(f32[4,128,128]{2,1,0:T(8,128)} %get-tuple-element.10), custom_call_target="InvertDiagBlocksLowerTriangular" | custom-call | tf_op jit(solution)/shard_map/triangular_solve | solution.py:74
  752.3 3.7 fusion.13
  756.0 3.7 convolution_subtract_fusion.2
  759.8 2.0 fusion.53
  761.8 2.6 convolution_subtract_fusion.1
  764.4 1.9 fusion.55
  766.3 4.0 fusion.7
  770.4 1.9 fusion.57
  772.3 3.5 fusion.6
  775.8 17.5 %convolution_subtract_fusion = f32[4096,512]{0,1:T(8,128)} fusion(f32[4096,512]{0,1:T(8,128)} %get-tuple-element.29, f32[128,4096]{1,0:T(8,128)S(1)} %fusion.57, f32[128,4096]{1,0:T(8,128)S(1)} %fusion.55, f32[128,4096]{1,0:T(8,128)S(1)} %fusion.53, f32[128,4096]{1,0:T(8,128)S(1)} %fusion.13, f32[128,512]{1,0:T(8,128)S(1)} %fusion.56, ...), kind=kOutput, calls=%fused_computation.10 | convolution fusion | flops 12894076928 | bytes 26214400 | tf_op jit(solution)/shard_map/dot_general | solution.py:77
  794.6 8.9 %copy.22 = f32[4096,512]{1,0:T(8,128)} copy(f32[4096,512]{0,1:T(8,128)} %fusion.6) | data formatting | bytes 16777216
  803.5 9.1 %copy.21 = f32[4096,512]{1,0:T(8,128)} copy(f32[4096,512]{0,1:T(8,128)} %convolution_subtract_fusion) | data formatting | bytes 16777216
  (93 shorter events, 25.4 us)
Async XLA Ops:
  7.2 1.6 copy-start
  7.2 152.3 %all-gather.2.cloned.1.call-start = ((), (), s32[]{:S(2)}) async-start(), calls=%async_computation.1 | async-start | bytes 17825792 | tf_op jit(solution)/shard_map/all_gather | solution.py:49
  26.3 336.7 %reduce-scatter.2.cloned.1.call-start = ((), (), s32[]{:S(2)}) async-start(), calls=%async_computation.2 | async-start | bytes 25165824 | tf_op jit(solution)/shard_map/reduce_scatter | solution.py:50
  175.5 367.1 %all-reduce.5.cloned.1.call-start = ((), (), s32[]{:S(2)}) async-start(), calls=%async_computation.3 | async-start | bytes 16777216 | tf_op jit(solution)/shard_map/psum | solution.py:15
  372.5 235.8 %all-reduce.7.cloned.1.call-start = ((), (), s32[]{:S(2)}) async-start(), calls=%async_computation.4 | async-start | bytes 4194304 | tf_op jit(solution)/shard_map/psum | solution.py:15
  608.3 1.7 copy-start.2
  695.0 52.4 %copy-start.3 = (f32[512,512]{0,1:T(8,128)S(1)}, f32[512,512]{0,1:T(8,128)}, u32[]{:S(2)}) copy-start(f32[512,512]{0,1:T(8,128)} %get-tuple-element.27) | copy-start | bytes 3145732
  751.9 9.9 %slice-start = ((s8[8388608]{0:T(1024)(128)(4,1)}), s8[4194304]{0:T(1024)(128)(4,1)S(1)}, s32[]{:S(2)}) async-start(s8[8388608]{0:T(1024)(128)(4,1)} %bitcast.118), calls=%async_computation.5 | async-start | bytes 8388608
  756.0 5.7 slice-start.1
  803.5 9.1 %copy-start.1 = (bf16[1024,1024]{1,0:T(8,128)(2,1)S(1)}, bf16[1024,1024]{1,0:T(8,128)(2,1)}, u32[]{:S(2)}) copy-start(bf16[1024,1024]{1,0:T(8,128)(2,1)} %param.7) | copy-start | bytes 6291460
Sparse Core Ops, SparseCore 0:
  26.4 133.0 all-gather.1
  175.6 187.2 reduce-scatter.1
  372.6 169.9 all-reduce.4
  545.4 62.9 all-reduce.6
where the time goes:
time: 828 us; the launch traced here: 820 us
  waiting for transfers between devices  514 us (62%)
  other arithmetic  140 us (17%)
  matrix products  80 us (10%)
  blocking collectives  36.2 us (4%)
  local copies, waits for them, and re-layouts  31.2 us (4%)
  between operations  17.9 us (2%)
    psum x2, waiting for transfers between devices, broadcast(): return lax.psum(jnp.where(mine, shard, jnp.zeros_like(shard)), axis)  194 us
    reduce_scatter x1, waiting for transfers between devices, per_device(): lax.psum_scatter(gram_part, 'samp', scatter_dimension=0, tiled=True)  187 us
    all_gather x1, waiting for transfers between devices, per_device(): lax.all_gather(feature_obs, 'feat', axis=1, tiled=True)  133 us
    another operation x14, other arithmetic, per_device(): lower = jnp.linalg.cholesky(pivot)  79.1 us
    another operation x3, other arithmetic, per_device(): lax.linalg.triangular_solve(lower, panel_cols.T, left_side=True, lower=True)  40.3 us
    psum x1, blocking collectives, broadcast(): return lax.psum(jnp.where(mine, shard, jnp.zeros_like(shard)), axis)  31.2 us
    another operation x7, matrix products, per_device(): lax.linalg.triangular_solve(lower, panel_cols.T, left_side=True, lower=True)  19.9 us
    unnamed x14, local copies, waits for them, and re-layouts  18.1 us
  transfers between devices with their start and end apart: 4, of which 4 were waited for; matrix products, arithmetic and copies ran while one was open for 0% of the time, Pallas kernels for 0%

commit v1 on v0

v1 whole, which is shorter than its diff:
```python
import functools

import jax
import jax.numpy as jnp
from jax import lax
from jax.experimental import pallas as pl
from jax.experimental.pallas import tpu as pltpu
from jax.sharding import PartitionSpec as P

PANEL = 512
TILE = 128
LANES = 128

ridge = 0.1
turn = 0.15915494309189535
magic = 12582912.0
VMEM_BYTES = 58 * 1024 * 1024
COS = (1.4142124462507522, -27.915133726537626, 91.8229879115028, -120.59228365935401, 83.14231129485714, -29.79904335273614)


def cosine_turns(u):
    whole = (u + magic) - magic
    frac = u - whole
    square = frac * frac
    acc = jnp.full_like(square, COS[-1])
    for coef in COS[-2::-1]:
        acc = acc * square + coef
    return acc


def feature_kernel(emb_ref, freq_ref, base_ref, full_ref, treated_ref, counter_ref, feat_ref, moment_ref):
    @pl.when(pl.program_id(0) == 0)
    def _():
        moment_ref[...] = jnp.zeros_like(moment_ref)

    scaled = jnp.dot(emb_ref[...], freq_ref[...], preferred_element_type=jnp.float32) * turn
    base, full = base_ref[...], full_ref[...]
    observed = cosine_turns(scaled + jnp.where(treated_ref[...] > 0.5, full, base))
    counterfactual = cosine_turns(scaled + jnp.where(counter_ref[...] > 0.5, full, base))
    feat_ref[...] = observed.astype(jnp.bfloat16)
    moment_ref[...] += jnp.sum(counterfactual - observed, axis=0, keepdims=True)


def make_features(emb, freq, base, full, treated, counter):
    count, emb_width = emb.shape
    width = freq.shape[1]
    step = 256
    whole = lambda shape: pl.BlockSpec(shape, lambda i: (0, 0))
    return pl.pallas_call(
        feature_kernel,
        grid=(count // step,),
        in_specs=[
            pl.BlockSpec((step, emb_width), lambda i: (i, 0)),
            whole((emb_width, width)),
            whole((1, width)),
            whole((1, width)),
            pl.BlockSpec((step, 1), lambda i: (i, 0)),
            pl.BlockSpec((step, 1), lambda i: (i, 0)),
        ],
        out_specs=[pl.BlockSpec((step, width), lambda i: (i, 0)), whole((1, width))],
        out_shape=[
            jax.ShapeDtypeStruct((count, width), jnp.bfloat16),
            jax.ShapeDtypeStruct((1, width), jnp.float32),
        ],
        cost_estimate=pl.CostEstimate(
            flops=2 * count * emb_width * width, bytes_accessed=2 * count * emb_width, transcendentals=2 * count * width
        ),
        compiler_params=pltpu.CompilerParams(vmem_limit_bytes=VMEM_BYTES),
    )(emb, freq, base, full, treated, counter)


def inverse_factor(tile):
    groups = TILE // 8
    sub = lax.broadcasted_iota(jnp.int32, (8, TILE), 0)
    lane = lax.broadcasted_iota(jnp.int32, (8, TILE), 1)
    left = [tile[8 * g : 8 * g + 8, :] for g in range(groups)]
    right = [jnp.where(lane == sub + 8 * g, 1.0, 0.0) for g in range(groups)]
    for j in range(TILE):
        g, t = divmod(j, 8)
        row = left[g][t : t + 1, :]
        scale = 1.0 / row[:, j : j + 1]
        left_row = row * scale
        right_row = right[g][t : t + 1, :] * scale
        for i in range(g, groups):
            col = left[i][:, j : j + 1]
            if i == g:
                col = jnp.where(sub[:, :1] > t, col, 0.0)
            left[i] = left[i] - col * left_row
            right[i] = right[i] - col * right_row
    out = []
    for g in range(groups):
        diag = jnp.sum(jnp.where(lane == sub + 8 * g, left[g], 0.0), axis=1, keepdims=True)
        out.append(right[g] * (1.0 / jnp.sqrt(diag)))
    return jnp.concatenate(out, axis=0)


def split(value):
    high = value.astype(jnp.bfloat16)
    return high, (value - high.astype(jnp.float32)).astype(jnp.bfloat16)


def solve_kernel(
    sample_count,
    shift_ref,
    pivot_ref,
    cross_ref,
    moment_ref,
    moment_panel_ref,
    inv_high_ref,
    inv_low_ref,
    cross_high_ref,
    cross_low_ref,
    reduced_ref,
    x_ref,
):
    width = cross_ref.shape[1]
    start = 2 * PANEL
    rows = lax.broadcasted_iota(jnp.int32, (PANEL, PANEL), 0)
    cols = lax.broadcasted_iota(jnp.int32, (PANEL, PANEL), 1)
    eye = jnp.where(rows == cols, 1.0, 0.0)
    x_ref[:, 0:PANEL] = pivot_ref[...] / sample_count + ridge * eye
    x_ref[:, PANEL:start] = eye
    rows = lax.broadcasted_iota(jnp.int32, (PANEL, width), 0)
    cols = lax.broadcasted_iota(jnp.int32, (PANEL, width), 1)
    own = jnp.where(rows == cols + shift_ref[0], ridge, 0.0)
    x_ref[:, start : start + width] = cross_ref[...] / sample_count + own
    column = jnp.sum(eye * (moment_panel_ref[...] / sample_count), axis=1, keepdims=True)
    x_ref[:, start + width :] = jnp.broadcast_to(column, (PANEL, LANES))

    def block(b, carry):
        at = pl.multiple_of(b * TILE, TILE)
        inverse = inverse_factor(x_ref[pl.ds(at, TILE), pl.ds(at, TILE)])
        solved = jnp.dot(inverse, x_ref[pl.ds(at, TILE), :], precision=lax.Precision.HIGHEST, preferred_element_type=jnp.float32)
        lanes = lax.broadcasted_iota(jnp.int32, (TILE, PANEL), 1)
        coef = jnp.where(lanes >= at + TILE, solved[:, :PANEL], 0.0)
        x_ref[...] -= jnp.dot(coef.T, solved, precision=lax.Precision.HIGHEST, preferred_element_type=jnp.float32)
        x_ref[pl.ds(at, TILE), :] = solved
        return carry

    lax.fori_loop(0, PANEL // TILE, block, 0)
    inv_high_ref[...], inv_low_ref[...] = split(x_ref[:, PANEL:start].T)
    cross = x_ref[:, start : start + width]
    cross_high_ref[...], cross_low_ref[...] = split(cross)
    solved = x_ref[:, start + width : start + width + 1]
    reduced = moment_ref[...] / sample_count - jnp.sum(cross * solved, axis=0, keepdims=True)
    reduced_ref[...] = jnp.sqrt(jnp.float32(sample_count)) * reduced


def eliminate(sample_count, shift, pivot, cross, moment, moment_panel):
    width = cross.shape[1]
    vmem = pl.BlockSpec(memory_space=pltpu.VMEM)
    square = jax.ShapeDtypeStruct((PANEL, PANEL), jnp.bfloat16)
    wide = jax.ShapeDtypeStruct((PANEL, width), jnp.bfloat16)
    return pl.pallas_call(
        functools.partial(solve_kernel, sample_count),
        in_specs=[pl.BlockSpec(memory_space=pltpu.SMEM)] + [vmem] * 4,
        out_specs=[vmem] * 5,
        out_shape=[square, square, wide, wide, jax.ShapeDtypeStruct((1, width), jnp.float32)],
        scratch_shapes=[pltpu.VMEM((PANEL, 2 * PANEL + width + LANES), jnp.float32)],
        cost_estimate=pl.CostEstimate(flops=40 * 10**9, bytes_accessed=4 * 10**6, transcendentals=0),
        compiler_params=pltpu.CompilerParams(vmem_limit_bytes=VMEM_BYTES),
    )(shift, pivot, cross, moment, moment_panel)


def three_pass(left, right_high, right_low):
    high, low = split(left)
    dot = functools.partial(jnp.dot, preferred_element_type=jnp.float32)
    return dot(high, right_high) + (dot(high, right_low) + dot(low, right_high))


def main_kernel(
    sample_count,
    order_ref,
    place_ref,
    freq_ref,
    base_ref,
    full_ref,
    emb_ref,
    treated_ref,
    feat_ref,
    feat_panel_ref,
    inv_high_ref,
    inv_low_ref,
    cross_high_ref,
    cross_low_ref,
    schur_ref,
    panel_ref,
):
    height = freq_ref.shape[0]
    count = emb_ref.shape[1]
    width = feat_ref.shape[1]
    base, full = base_ref[...], full_ref[...]
    own = jnp.zeros((height, width), jnp.float32)
    panel = jnp.zeros((height, PANEL), jnp.float32)
    step = 512
    for at in range(0, count, step):
        scaled = jnp.dot(freq_ref[...], emb_ref[:, at : at + step], preferred_element_type=jnp.float32) * turn
        phase = jnp.where(treated_ref[:, at : at + step] > 0.5, full, base)
        features = cosine_turns(scaled + phase).astype(jnp.bfloat16)
        own += jnp.dot(features, feat_ref[at : at + step, :], preferred_element_type=jnp.float32)
        panel += jnp.dot(features, feat_panel_ref[at : at + step, :], preferred_element_type=jnp.float32)
    first = place_ref[0] + order_ref[pl.program_id(0)] * height
    rows = first + lax.broadcasted_iota(jnp.int32, (height, width), 0)
    cols = place_ref[1] + lax.broadcasted_iota(jnp.int32, (height, width), 1)
    own = own / sample_count + jnp.where(rows == cols, ridge, 0.0)
    rows = first + lax.broadcasted_iota(jnp.int32, (height, PANEL), 0)
    cols = place_ref[2] + lax.broadcasted_iota(jnp.int32, (height, PANEL), 1)
    panel = panel / sample_count + jnp.where(rows == cols, ridge, 0.0)
    factor = three_pass(panel, inv_high_ref[...], inv_low_ref[...])
    panel_ref[...] = factor
    schur_ref[...] = own - three_pass(factor, cross_high_ref[...], cross_low_ref[...])


def main(order, place, freqs, base, full, emb_t, treated, feat, feat_panel, solved):
    blocks = order.shape[0]
    row_height, emb_width = freqs.shape
    height = row_height // blocks
    count, width = feat.shape
    fixed = lambda array: pl.BlockSpec(array.shape, lambda i, order, place: (0, 0), pipeline_mode=pl.Buffered(1))
    moved = lambda cols: pl.BlockSpec((height, cols), lambda i, order, place: (order[i], 0))
    flops = 2 * row_height * (count * (emb_width + width + PANEL) + 3 * PANEL * (PANEL + width))
    return pl.pallas_call(
        functools.partial(main_kernel, count),
        grid_spec=pltpu.PrefetchScalarGridSpec(
            num_scalar_prefetch=2,
            grid=(blocks,),
            in_specs=[
                pl.BlockSpec((height, emb_width), lambda i, order, place: (i, 0)),
                moved(1),
                moved(1),
                fixed(emb_t),
                fixed(treated),
                fixed(feat),
                fixed(feat_panel),
            ]
            + [fixed(array) for array in solved],
            out_specs=[moved(width), moved(PANEL)],
        ),
        out_shape=[
            jax.ShapeDtypeStruct((row_height, width), jnp.float32),
            jax.ShapeDtypeStruct((row_height, PANEL), jnp.float32),
        ],
        cost_estimate=pl.CostEstimate(flops=flops, bytes_accessed=30 * 10**6, transcendentals=count * row_height),
        compiler_params=pltpu.CompilerParams(vmem_limit_bytes=VMEM_BYTES),
    )(order, place, freqs, base, full, emb_t, treated, feat, feat_panel, *solved)


def gather_rows_staged(freq_t, samp_index, feat_index):
    half = 8
    mates = [(s * 16 + f, s * 16 + (f ^ half)) for s in range(2) for f in range(s * half, (s + 1) * half)]

    def swap(value, bits):
        return lax.ppermute(value, "feat", [(f, f ^ bits) for f in range(16)])

    crossed = lax.ppermute(freq_t, ("samp", "feat"), mates)
    mine = jnp.where(feat_index // half == samp_index, freq_t, crossed)
    near = [mine, swap(mine, 4), swap(mine, 2), swap(mine, 6)]
    other = [swap(block, 1) for block in near]
    order = jnp.bitwise_xor(feat_index % half, jnp.array([0, 4, 2, 6, 1, 5, 3, 7], jnp.int32))
    return jnp.concatenate(near + other, axis=0), order


def gather_samples_staged(embeddings, marks, samp_index, feat_index):
    part = embeddings.shape[0] // 2
    core = feat_index % 2
    mine = lax.dynamic_slice_in_dim(embeddings, core * part, part, 0)
    got = lax.ppermute(mine, "samp", [(0, 1), (1, 0)])
    got_mate = lax.ppermute(got, "feat", [(f, f ^ 1) for f in range(16)])
    lower = jnp.where(core == 0, got, got_mate)
    upper = jnp.where(core == 0, got_mate, got)
    other = jnp.concatenate([lower, upper], axis=0)
    first = samp_index == 0
    emb = jnp.concatenate([jnp.where(first, embeddings, other), jnp.where(first, other, embeddings)], axis=0)
    other_marks = lax.ppermute(marks, "samp", [(0, 1), (1, 0)])
    marks = jnp.concatenate(
        [jnp.where(first, marks, other_marks), jnp.where(first, other_marks, marks)], axis=1
    )
    return emb, marks


def per_device(embeddings, frequencies, phases, treat_freq, treatment, flips, panel):
    samp_size = lax.axis_size("samp")
    feat_size = lax.axis_size("feat")
    samp_index = lax.axis_index("samp")
    feat_index = lax.axis_index("feat")
    emb_width, col_width = frequencies.shape
    feat_total = col_width * feat_size
    row_height = feat_total // samp_size
    first_col = panel[0] * PANEL
    first_dev = first_col // col_width
    staged = samp_size == 2 and feat_size == 16

    panel_freq = []
    for member in range(PANEL // col_width):
        own = feat_index == first_dev + member
        panel_freq.append(lax.psum(jnp.where(own, frequencies, jnp.zeros_like(frequencies)), "feat"))
    panel_freq = jnp.concatenate(panel_freq, axis=1)

    treated = treatment.astype(jnp.float32)
    flipped = flips.astype(jnp.float32)
    counter = treated + flipped - 2.0 * treated * flipped
    marks = jnp.stack([treated, counter])
    base_own = phases * turn
    turns = lax.all_gather(jnp.stack([base_own, base_own + treat_freq * turn]), "feat", axis=1, tiled=True)
    if staged:
        emb, marks = gather_samples_staged(embeddings, marks, samp_index, feat_index)
        freqs, order = gather_rows_staged(frequencies.T, samp_index, feat_index)
    else:
        emb = lax.all_gather(embeddings, "samp", axis=0, tiled=True)
        marks = lax.all_gather(marks, "samp", axis=1, tiled=True)
        freqs = lax.all_gather(frequencies.T, "feat", axis=0, tiled=True)
        freqs = lax.dynamic_slice_in_dim(freqs, samp_index * row_height, row_height, 0)
        order = jnp.arange(row_height // col_width, dtype=jnp.int32)
    treated_col, counter_col = marks[0][:, None], marks[1][:, None]
    count = emb.shape[0]

    own_turns = lax.dynamic_slice_in_dim(turns, feat_index * col_width, col_width, 1)
    panel_turns = lax.dynamic_slice_in_dim(turns, first_col, PANEL, 1)
    row_turns = lax.dynamic_slice_in_dim(turns, samp_index * row_height, row_height, 1)
    feat, moment = make_features(emb, frequencies, own_turns[:1], own_turns[1:], treated_col, counter_col)
    feat_panel, moment_panel = make_features(
        emb, panel_freq, panel_turns[:1], panel_turns[1:], treated_col, counter_col
    )
    inner = lambda left, right: lax.dot_general(
        left, right, (((0,), (0,)), ((), ())), preferred_element_type=jnp.float32
    )
    pivot = inner(feat_panel, feat_panel)
    cross = inner(feat_panel, feat)
    own_col = feat_index * col_width
    shift = (own_col - first_col).reshape(1).astype(jnp.int32)
    *solved, reduced = eliminate(count, shift, pivot, cross, moment, moment_panel)
    place = jnp.stack([samp_index * row_height, own_col, first_col]).astype(jnp.int32)
    schur, panel_factor = main(
        order,
        place,
        freqs,
        row_turns[0][:, None],
        row_turns[1][:, None],
        emb.T,
        marks[:1],
        feat,
        feat_panel,
        solved,
    )
    return schur, panel_factor, reduced[0]


def solution(mesh):
    return jax.shard_map(
        per_device,
        mesh=mesh,
        in_specs=(
            P("samp", None),
            P(None, "feat"),
            P("feat"),
            P("feat"),
            P("samp"),
            P("samp"),
            P(),
        ),
        out_specs=(P("samp", "feat"), P("samp", None), P("feat")),
        check_vma=False,
    )
```

time: 828 us -> 330 us (0.40)
  waiting for transfers between devices: 514 us -> 40 us
  Pallas kernels: 0 us -> 150 us
  other arithmetic: 140 us -> 12.5 us
  matrix products: 80 us -> 6.86 us
  starting transfers between devices: 0.16 us -> 33.3 us
    reduce_scatter x1 -> x0, waiting for transfers between devices: 187 us -> none  [per_device(): lax.psum_scatter(gram_part, 'samp', scatter_dimension=0, tiled=True)]
    psum x2 -> x1, waiting for transfers between devices: 194 us -> 15.5 us  [per_device(): lax.psum(jnp.where(own, frequencies, jnp.zeros_like(frequencies)), 'feat')]
    pallas_call x0 -> x4, Pallas kernels: none -> 150 us  [the longest x1 67.1 us: main(): pl.pallas_call(functools.partial(main_kernel, count), grid_spec=pltpu.Pre...]
    all_gather x1 -> x0, waiting for transfers between devices: 133 us -> none  [per_device(): lax.all_gather(feature_obs, 'feat', axis=1, tiled=True)]
    another operation x17 -> x4, other arithmetic: 119 us -> 0.69 us  [the longest x1 0.65 us: per_device(): jnp.stack([samp_index * row_height, own_col, first_col]).astype(jnp.int32)]
    dot_general x4 -> x2, matrix products: 51.6 us -> 6.86 us  [per_device(): lax.dot_general(left, right, (((0,), (0,)), ((), ())), preferred_element_...]
    all_gather x0 -> x1, blocking collectives: none -> 40.4 us  [per_device(): lax.all_gather(jnp.stack([base_own, base_own + treat_freq * turn]), 'feat...]
    psum x2 -> x0, blocking collectives: 36.2 us -> none  [the longest x1 31.2 us: broadcast(): return lax.psum(jnp.where(mine, shard, jnp.zeros_like(shard)), axis)]
  transfers between devices with their start and end apart: 4 -> 12, of which waited for: 4 -> 3; matrix products, arithmetic and copies ran while one was open for 0% -> 14% of each run, Pallas kernels for 0% -> 25%
where the time goes in v1:
time: 330 us; the launch traced here: 329 us
  Pallas kernels  150 us (45%)
  blocking collectives  40.4 us (12%)
  waiting for transfers between devices  40 us (12%)
  starting transfers between devices  33.3 us (10%)
  local copies, waits for them, and re-layouts  30.4 us (9%)
  between operations  14.9 us (5%)
  other arithmetic  12.5 us (4%)
  matrix products  6.86 us (2%)
    pallas_call x1, Pallas kernels, main(): pl.pallas_call(functools.partial(main_kernel, count), grid_spec=pltpu.Pre...  67.1 us
    pallas_call x1, Pallas kernels, eliminate(): pl.pallas_call(functools.partial(solve_kernel, sample_count), in_specs=[p...  61.3 us
    all_gather x1, blocking collectives, per_device(): lax.all_gather(jnp.stack([base_own, base_own + treat_freq * turn]), 'feat...  40.4 us
    ppermute x7, waiting for transfers between devices, swap(): return lax.ppermute(value, 'feat', [(f, f ^ bits) for f in range(16)])  24.5 us
    ppermute x7, starting transfers between devices, swap(): return lax.ppermute(value, 'feat', [(f, f ^ bits) for f in range(16)])  23.9 us
    pallas_call x2, Pallas kernels, make_features(): pl.pallas_call(feature_kernel, grid=(count // step,), in_specs=[pl.BlockS...  21.9 us
    psum x1, waiting for transfers between devices, per_device(): lax.psum(jnp.where(own, frequencies, jnp.zeros_like(frequencies)), 'feat')  15.5 us
    unnamed x22, local copies, waits for them, and re-layouts  14.4 us
  transfers between devices with their start and end apart: 12, of which 3 were waited for; matrix products, arithmetic and copies ran while one was open for 14% of the time, Pallas kernels for 25%

profile of v1, /device:TPU:0, one launch (start us, length us, event | category | flops | bytes accessed | tf_op | source)
XLA Modules:
  0.0 328.6 jit_solution(2539186561606958023)
XLA Ops:
  8.7 3.0 collective-permute-start.10
  11.7 2.9 copy.19
  14.6 1.1 constant_dynamic-slice_fusion.2
  16.4 1.1 broadcast_select_fusion.2
  17.5 1.5 copy.17
  19.0 6.0 %collective-permute-start = (bf16[512,1024]{1,0:T(8,128)(2,1)S(1)}, bf16[512,1024]{1,0:T(8,128)(2,1)}, u32[]{:S(2)}, u32[]{:S(2)}) collective-permute-start(bf16[512,1024]{1,0:T(8,128)(2,1)S(1)} %bitcast.25), channel_id=1, source_target_pairs={{0,8},{1,9},{2,10},{3,11},{4,12},{5,13},{6,14},{7,15},{24,16},{25,... | collective-permute-start | bytes 3145736 | tf_op jit(solution)/shard_map/ppermute | solution.py:255
  25.0 40.4 %all_gather.3 = f32[2,8192]{1,0:T(2,128)S(1)} all-gather(f32[2,512]{1,0:T(2,128)S(1)} %pad_maximum_fusion.4), channel_id=1, replica_groups=mesh['samp'=2,'feat'=16] {'feat'}, dimensions={1}, use_global_device_ids=true | all-gather | bytes 69632 | tf_op jit(solution)/shard_map/all_gather | solution.py:304
  67.8 2.0 copy.28.full_ref
  69.8 2.0 copy.27.base_ref
  71.8 1.4 copy.23.counter_ref
  73.2 1.4 copy.22.treated_ref
  74.6 1.9 constant_dynamic-update-slice_fusion.7
  76.6 23.1 %collective-permute-start.3 = (bf16[512,1024]{1,0:T(8,128)(2,1)}, bf16[512,1024]{1,0:T(8,128)(2,1)S(1)}, u32[]{:S(2)}, u32[]{:S(2)}) collective-permute-start(bf16[512,1024]{1,0:T(8,128)(2,1)} %get-tuple-element.26), channel_id=1, source_target_pairs={{0,6},{1,7},{2,4},{3,5},{4,2},{5,3},{6,0},{7,1},{8,14},{9,15},{10,... | collective-permute-start | bytes 3145736 | tf_op jit(solution)/shard_map/ppermute | solution.py:253
  100.3 1.7 broadcast_select_fusion.4
  102.0 1.0 broadcast_select_fusion.1
  103.0 4.1 %pad_maximum_fusion = (bf16[2048,1024]{0,1:T(8,128)(2,1)}, bf16[1024,2048]{1,0:T(8,128)(2,1)}) fusion(bf16[1024,1024]{0,1:T(8,128)(2,1)S(1)} %get-tuple-element.30, bf16[1024,1024]{0,1:T(8,128)(2,1)S(1)} %get-tuple-element.29), kind=kLoop, calls=%fused_computation | loop fusion | flops 8388608 | bytes 12582912 | tf_op jit(solution)/shard_map/concatenate | solution.py:273
  107.1 6.4 %copy.21.emb_ref = bf16[2048,1024]{1,0:T(8,128)(2,1)} copy(bf16[2048,1024]{0,1:T(8,128)(2,1)} %get-tuple-element.27) | data formatting | bytes 8388608 | tf_op jit(solution)/shard_map/concatenate | solution.py:273
  113.5 11.0 %shard_map.103 = (bf16[2048,512]{1,0:T(8,128)(2,1)}, f32[1,512]{1,0:T(1,128)}) custom-call(bf16[2048,1024]{1,0:T(8,128)(2,1)} %copy.21.emb_ref, bf16[1024,512]{1,0:T(8,128)(2,1)} %freq_ref.1, f32[1,512]{1,0:T(1,128)} %get-tuple-element.35.base_ref, f32[1,512]{1,0:T(1,128)} %get-tuple-element.36.full_ref, f32[2048,1]{1,0:T(8,128)} %copy.22.treated_ref, ...), custom_call_target="tpu_custom_call" | custom-call | flops 2147483648 | bytes 4194304 | tf_op jit(solution)/shard_map/pallas_call | solution.py:49
  124.6 24.4 %collective-permute-done.2 = bf16[512,1024]{1,0:T(8,128)(2,1)} collective-permute-done((bf16[512,1024]{1,0:T(8,128)(2,1)}, bf16[512,1024]{1,0:T(8,128)(2,1)}, u32[]{:S(2)}, u32[]{:S(2)}) %collective-permute-start.2) | collective-permute-done | bytes 1048608 | tf_op jit(solution)/shard_map/ppermute | solution.py:253
  149.0 15.5 %all-reduce.2.cloned.1.call-done.freq_ref = bf16[1024,512]{1,0:T(8,128)(2,1)} async-done(((bf16[1024,512]{1,0:T(8,128)(2,1)}), bf16[1024,512]{1,0:T(8,128)(2,1)}) %all-reduce.2.cloned.1.call-update) | async-done | bytes 1048592 | tf_op jit(solution)/shard_map/psum | solution.py:296
  164.5 10.9 %shard_map.104 = (bf16[2048,512]{1,0:T(8,128)(2,1)}, f32[1,512]{1,0:T(1,128)}) custom-call(bf16[2048,1024]{1,0:T(8,128)(2,1)} %copy.21.emb_ref, bf16[1024,512]{1,0:T(8,128)(2,1)} %all-reduce.2.cloned.1.call-done.freq_ref, f32[1,512]{1,0:T(1,128)} %get-tuple-element.34.base_ref, f32[1,512]{1,0:T(1,128)} %get-tuple-element.33.full_ref, ...), custom_call_target="tpu_custom_call" | custom-call | flops 2147483648 | bytes 4194304 | tf_op jit(solution)/shard_map/pallas_call | solution.py:49
  175.5 4.6 %fusion.4.pivot_ref = f32[512,512]{1,0:T(8,128)} fusion(bf16[2048,512]{1,0:T(8,128)(2,1)} %get-tuple-element.15.feat_panel_ref), kind=kOutput, calls=%fused_computation.37 | convolution fusion | flops 1073741824 | bytes 3145728 | tf_op jit(solution)/shard_map/dot_general | solution.py:324
  180.1 2.2 fusion.5.cross_ref
  182.3 61.3 %shard_map.105 = (bf16[512,512]{1,0:T(8,128)(2,1)}, bf16[512,512]{1,0:T(8,128)(2,1)}, bf16[512,512]{1,0:T(8,128)(2,1)}, bf16[512,512]{1,0:T(8,128)(2,1)}, f32[1,512]{1,0:T(1,128)}) custom-call(s32[1]{0:T(128)} %bitcast.13.shift_ref, f32[512,512]{1,0:T(8,128)} %fusion.4.pivot_ref, f32[512,512]{1,0:T(8,128)} %fusion.5.cross_ref, ...), custom_call_target="tpu_custom_call" | custom-call | flops 40000000000 | bytes 4000000 | tf_op jit(solution)/shard_map/pallas_call | solution.py:154
  243.6 2.3 constant_dynamic-update-slice_fusion.6
  245.8 2.3 constant_dynamic-update-slice_fusion.5
  248.1 1.0 constant_dynamic-update-slice_fusion.4
  249.2 2.3 constant_dynamic-update-slice_fusion.3
  251.5 1.1 constant_dynamic-update-slice_fusion.2
  252.5 1.0 constant_dynamic-update-slice_fusion.1
  253.6 1.1 constant_dynamic-update-slice_fusion.freq_ref
  254.7 67.1 %shard_map.106 = (f32[4096,512]{1,0:T(8,128)}, f32[4096,512]{1,0:T(8,128)}) custom-call(s32[8]{0:T(128)} %broadcast_xor_fusion.order_ref, s32[3]{0:T(128)} %pad_add_fusion.place_ref, bf16[4096,1024]{1,0:T(8,128)(2,1)} %constant_dynamic-update-slice_fusion.freq_ref, f32[4096,1]{1,0:T(8,128)} %copy.27.base_ref, f32[4096,1]{1,0:T(8,128)} %copy.28.full_ref, ...), custom_call_target="tpu_custom_call" | custom-call | flops 47244640256 | bytes 30000000 | tf_op jit(solution)/shard_map/pallas_call | solution.py:222
  (45 shorter events, 5.0 us)
Async XLA Ops:
  7.2 9.3 %copy-start = (bf16[1024,512]{1,0:T(8,128)(2,1)S(1)}, bf16[1024,512]{1,0:T(8,128)(2,1)}, u32[]{:S(2)}) copy-start(bf16[1024,512]{1,0:T(8,128)(2,1)} %freq_ref.1) | copy-start | bytes 3145732
  7.2 157.3 %all-reduce.2.cloned.1.call-start = ((), (), s32[]{:S(2)}) async-start(), calls=%async_computation | async-start | bytes 2097152 | tf_op jit(solution)/shard_map/psum | solution.py:296
  8.7 63.0 %collective-permute-start.10 = (f32[2,1024]{1,0:T(2,128)S(1)}, f32[2,1024]{1,0:T(2,128)S(1)}, u32[]{:S(2)}, u32[]{:S(2)}) collective-permute-start(f32[2,1024]{1,0:T(2,128)S(1)} %pad_maximum_fusion.3), channel_id=1, source_target_pairs={{0,16},{16,0},{1,17},{17,1},{2,18},{18,2},{3,19},{19,3},{4,20},{20... | collective-permute-start | bytes 24584 | tf_op jit(solution)/shard_map/ppermute | solution.py:274
  14.6 10.4 %copy-start.2 = (f32[512]{0:T(512)S(1)}, f32[512]{0:T(512)}, u32[]{:S(2)}) copy-start(f32[512]{0:T(512)} %param.10) | copy-start | bytes 6148
  14.6 10.4 %copy-start.3 = (f32[512]{0:T(512)S(1)}, f32[512]{0:T(512)}, u32[]{:S(2)}) copy-start(f32[512]{0:T(512)} %param.11) | copy-start | bytes 6148
  14.6 51.4 %copy-start.4 = (s32[8]{0:T(128)S(1)}, s32[8]{0:T(128)}, u32[]{:S(2)}) copy-start(s32[8]{0:T(128)} %constant.73.clone) | copy-start | bytes 100
  15.7 49.9 %collective-permute-start.8 = (bf16[512,1024]{0,1:T(8,128)(2,1)}, bf16[512,1024]{0,1:T(8,128)(2,1)}, u32[]{:S(2)}, u32[]{:S(2)}) collective-permute-start(bf16[512,1024]{0,1:T(8,128)(2,1)} %constant_dynamic-slice_fusion.2), channel_id=1, source_target_pairs={{0,16},{16,0},{1,17},{17,1},{2,18},{18,2},{3,19},{19,3},{4,20},{20... | collective-permute-start | bytes 3145736 | tf_op jit(solution)/shard_map/ppermute | solution.py:267
  19.0 55.5 %collective-permute-start = (bf16[512,1024]{1,0:T(8,128)(2,1)S(1)}, bf16[512,1024]{1,0:T(8,128)(2,1)}, u32[]{:S(2)}, u32[]{:S(2)}) collective-permute-start(bf16[512,1024]{1,0:T(8,128)(2,1)S(1)} %bitcast.25), channel_id=1, source_target_pairs={{0,8},{1,9},{2,10},{3,11},{4,12},{5,13},{6,14},{7,15},{24,16},{25,... | collective-permute-start | bytes 3145736 | tf_op jit(solution)/shard_map/ppermute | solution.py:255
  65.6 34.7 %collective-permute-start.9 = (bf16[512,1024]{0,1:T(8,128)(2,1)}, bf16[512,1024]{0,1:T(8,128)(2,1)}, u32[]{:S(2)}, u32[]{:S(2)}) collective-permute-start(bf16[512,1024]{0,1:T(8,128)(2,1)} %collective-permute-done.8), channel_id=1, source_target_pairs={{0,1},{1,0},{2,3},{3,2},{4,5},{5,4},{6,7},{7,6},{8,9},{9,8},{10,11... | collective-permute-start | bytes 3145736 | tf_op jit(solution)/shard_map/ppermute | solution.py:268
  71.8 30.2 %copy-start.1 = (f32[1,2048]{1,0:T(1,128)}, f32[1,2048]{1,0:T(1,128)S(1)}, u32[]{:S(2)}) copy-start(f32[1,2048]{1,0:T(1,128)S(1)} %get-tuple-element.40.treated_ref) | copy-start | bytes 24580
  76.4 172.7 %collective-permute-start.4 = (bf16[512,1024]{1,0:T(8,128)(2,1)}, bf16[512,1024]{1,0:T(8,128)(2,1)}, u32[]{:S(2)}, u32[]{:S(2)}) collective-permute-start(bf16[512,1024]{1,0:T(8,128)(2,1)} %get-tuple-element.26), channel_id=1, source_target_pairs={{0,1},{1,0},{2,3},{3,2},{4,5},{5,4},{6,7},{7,6},{8,9},{9,8},{10,11... | collective-permute-start | bytes 3145736 | tf_op jit(solution)/shard_map/ppermute | solution.py:253
  76.6 48.0 %collective-permute-start.3 = (bf16[512,1024]{1,0:T(8,128)(2,1)}, bf16[512,1024]{1,0:T(8,128)(2,1)S(1)}, u32[]{:S(2)}, u32[]{:S(2)}) collective-permute-start(bf16[512,1024]{1,0:T(8,128)(2,1)} %get-tuple-element.26), channel_id=1, source_target_pairs={{0,6},{1,7},{2,4},{3,5},{4,2},{5,3},{6,0},{7,1},{8,14},{9,15},{10,... | collective-permute-start | bytes 3145736 | tf_op jit(solution)/shard_map/ppermute | solution.py:253
  99.7 49.3 %collective-permute-start.2 = (bf16[512,1024]{1,0:T(8,128)(2,1)}, bf16[512,1024]{1,0:T(8,128)(2,1)}, u32[]{:S(2)}, u32[]{:S(2)}) collective-permute-start(bf16[512,1024]{1,0:T(8,128)(2,1)} %get-tuple-element.26), channel_id=1, source_target_pairs={{0,2},{1,3},{2,0},{3,1},{4,6},{5,7},{6,4},{7,5},{8,10},{9,11},{10,... | collective-permute-start | bytes 3145736 | tf_op jit(solution)/shard_map/ppermute | solution.py:253
  99.7 82.6 %collective-permute-start.1 = (bf16[512,1024]{1,0:T(8,128)(2,1)}, bf16[512,1024]{1,0:T(8,128)(2,1)}, u32[]{:S(2)}, u32[]{:S(2)}) collective-permute-start(bf16[512,1024]{1,0:T(8,128)(2,1)} %get-tuple-element.26), channel_id=1, source_target_pairs={{0,4},{1,5},{2,6},{3,7},{4,0},{5,1},{6,2},{7,3},{8,12},{9,13},{10,... | collective-permute-start | bytes 3145736 | tf_op jit(solution)/shard_map/ppermute | solution.py:253
  124.6 129.0 %collective-permute-start.7 = (bf16[512,1024]{1,0:T(8,128)(2,1)S(1)}, bf16[512,1024]{1,0:T(8,128)(2,1)S(1)}, u32[]{:S(2)}, u32[]{:S(2)}) collective-permute-start(bf16[512,1024]{1,0:T(8,128)(2,1)S(1)} %collective-permute-done.3), channel_id=1, source_target_pairs={{0,1},{1,0},{2,3},{3,2},{4,5},{5,4},{6,7},{7,6},{8,9},{9,8},{10,11... | collective-permute-start | bytes 3145736 | tf_op jit(solution)/shard_map/ppermute | solution.py:253
  149.0 103.6 %collective-permute-start.6 = (bf16[512,1024]{1,0:T(8,128)(2,1)}, bf16[512,1024]{1,0:T(8,128)(2,1)S(1)}, u32[]{:S(2)}, u32[]{:S(2)}) collective-permute-start(bf16[512,1024]{1,0:T(8,128)(2,1)} %collective-permute-done.2), channel_id=1, source_target_pairs={{0,1},{1,0},{2,3},{3,2},{4,5},{5,4},{6,7},{7,6},{8,9},{9,8},{10,11... | collective-permute-start | bytes 3145736 | tf_op jit(solution)/shard_map/ppermute | solution.py:253
  175.5 4.6 %copy-start.5 = (bf16[2048,512]{1,0:T(8,128)(2,1)S(1)}, bf16[2048,512]{1,0:T(8,128)(2,1)}, u32[]{:S(2)}) copy-start(bf16[2048,512]{1,0:T(8,128)(2,1)} %get-tuple-element.14.feat_ref) | copy-start | bytes 6291460
  175.5 4.6 %copy-start.6 = (bf16[2048,512]{1,0:T(8,128)(2,1)S(1)}, bf16[2048,512]{1,0:T(8,128)(2,1)}, u32[]{:S(2)}) copy-start(bf16[2048,512]{1,0:T(8,128)(2,1)} %get-tuple-element.15.feat_panel_ref) | copy-start | bytes 6291460
  182.3 69.1 %collective-permute-start.5 = (bf16[512,1024]{1,0:T(8,128)(2,1)}, bf16[512,1024]{1,0:T(8,128)(2,1)S(1)}, u32[]{:S(2)}, u32[]{:S(2)}) collective-permute-start(bf16[512,1024]{1,0:T(8,128)(2,1)} %collective-permute-done.1), channel_id=1, source_target_pairs={{0,1},{1,0},{2,3},{3,2},{4,5},{5,4},{6,7},{7,6},{8,9},{9,8},{10,11... | collective-permute-start | bytes 3145736 | tf_op jit(solution)/shard_map/ppermute | solution.py:253
Sparse Core Ops, SparseCore 0:
  17.7 146.8 all-reduce.1

commit v2 on v1

v2 whole, which is shorter than its diff:
```python
import functools

import jax
import jax.numpy as jnp
from jax import lax
from jax.experimental import pallas as pl
from jax.experimental.pallas import tpu as pltpu
from jax.sharding import PartitionSpec as P

PANEL = 512
TILE = 128
LANES = 128

ridge = 0.1
turn = 0.15915494309189535
magic = 12582912.0
VMEM_BYTES = 58 * 1024 * 1024
COS = (1.4142124462507522, -27.915133726537626, 91.8229879115028, -120.59228365935401, 83.14231129485714, -29.79904335273614)


def cosine_turns(u):
    whole = (u + magic) - magic
    frac = u - whole
    square = frac * frac
    acc = jnp.full_like(square, COS[-1])
    for coef in COS[-2::-1]:
        acc = acc * square + coef
    return acc


def split(value):
    high = value.astype(jnp.bfloat16)
    return high, (value - high.astype(jnp.float32)).astype(jnp.bfloat16)


def thirds(value):
    high = lax.reduce_precision(value, 8, 7)
    middle = lax.reduce_precision(value - high, 8, 7)
    low = value - high - middle
    return [part.astype(jnp.bfloat16) for part in (high, middle, low)]


def feature_kernel(pos_ref, emb_ref, freq_ref, treated_ref, counter_ref, feat_ref, moment_ref):
    @pl.when(pl.program_id(0) == 0)
    def _():
        moment_ref[...] = jnp.zeros_like(moment_ref)

    width = emb_ref.shape[1]
    parts = [freq_ref[width + k : width + k + 1, :].astype(jnp.float32) for k in range(6)]
    base = (parts[0] + parts[1]) + parts[2]
    full = (parts[3] + parts[4]) + parts[5]
    scaled = jnp.dot(emb_ref[...], freq_ref[:width, :], preferred_element_type=jnp.float32) * turn
    observed = cosine_turns(scaled + jnp.where(treated_ref[...] > 0.5, full, base))
    counterfactual = cosine_turns(scaled + jnp.where(counter_ref[...] > 0.5, full, base))
    feat_ref[...] = observed.astype(jnp.bfloat16)
    moment_ref[...] += jnp.sum(counterfactual - observed, axis=0, keepdims=True)


def make_features(pos, emb, freq, treated, counter):
    count, emb_width = emb.shape
    rows, width = freq.shape
    step = 256
    ratio = count // pos.shape[0] // step
    whole = lambda shape: pl.BlockSpec(shape, lambda i, pos: (0, 0))
    return pl.pallas_call(
        feature_kernel,
        grid_spec=pltpu.PrefetchScalarGridSpec(
            num_scalar_prefetch=1,
            grid=(count // step,),
            in_specs=[
                pl.BlockSpec((step, emb_width), lambda i, pos: (pos[i // ratio] * ratio + i % ratio, 0)),
                whole((rows, width)),
                pl.BlockSpec((step, 1), lambda i, pos: (i, 0)),
                pl.BlockSpec((step, 1), lambda i, pos: (i, 0)),
            ],
            out_specs=[pl.BlockSpec((step, width), lambda i, pos: (i, 0)), whole((1, width))],
        ),
        out_shape=[
            jax.ShapeDtypeStruct((count, width), jnp.bfloat16),
            jax.ShapeDtypeStruct((1, width), jnp.float32),
        ],
        cost_estimate=pl.CostEstimate(
            flops=2 * count * emb_width * width, bytes_accessed=2 * count * emb_width, transcendentals=2 * count * width
        ),
        compiler_params=pltpu.CompilerParams(vmem_limit_bytes=VMEM_BYTES),
    )(pos, emb, freq, treated, counter)


def inverse_factor(tile):
    groups = TILE // 8
    at_once = 4
    sub = lax.broadcasted_iota(jnp.int32, (8, TILE), 0)
    lane = lax.broadcasted_iota(jnp.int32, (8, TILE), 1)
    left = [tile[8 * g : 8 * g + 8, :] for g in range(groups)]
    right = [jnp.where(lane == sub + 8 * g, 1.0, 0.0) for g in range(groups)]
    spread = lambda value: jnp.broadcast_to(value, (8, TILE))
    for j in range(0, TILE, at_once):
        g, t = divmod(j, 8)
        ks = range(at_once)
        rows = [spread(left[g][t + k : t + k + 1, :]) for k in ks]
        marks = [spread(right[g][t + k : t + k + 1, :]) for k in ks]
        p = {(k, m): spread(rows[k][:, j + m : j + m + 1]) for k in ks for m in range(k, at_once)}
        f, inv = {}, []
        for k in ks:
            inv.append(1.0 / p[k, k])
            for m in range(k + 1, at_once):
                f[m, k] = p[k, m] * inv[k]
            for m in range(k + 1, at_once):
                for n in range(m, at_once):
                    p[m, n] = p[m, n] - f[m, k] * p[k, n]
        for k in ks:
            for q in range(k):
                rows[k] = rows[k] - f[k, q] * rows[q]
                marks[k] = marks[k] - f[k, q] * marks[q]
        row_part, mark_part = [None] * at_once, [None] * at_once
        for k in reversed(ks):
            row_part[k] = rows[k] * inv[k]
            mark_part[k] = marks[k] * inv[k]
            for q in range(k + 1, at_once):
                row_part[k] = row_part[k] - f[q, k] * row_part[q]
                mark_part[k] = mark_part[k] - f[q, k] * mark_part[q]
        for i in range(g, groups):
            if i > g or t + at_once < 8:
                cols = [spread(left[i][:, j + k : j + k + 1]) for k in ks]
                if i == g:
                    cols = [jnp.where(sub >= t + at_once, col, 0.0) for col in cols]
                left_sum = (cols[0] * row_part[0] + cols[1] * row_part[1]) + (cols[2] * row_part[2] + cols[3] * row_part[3])
                right_sum = (cols[0] * mark_part[0] + cols[1] * mark_part[1]) + (cols[2] * mark_part[2] + cols[3] * mark_part[3])
                left[i] = left[i] - left_sum
                right[i] = right[i] - right_sum
        for k in ks:
            left[g] = jnp.where(sub == t + k, rows[k], left[g])
            right[g] = jnp.where(sub == t + k, marks[k], right[g])
    out = []
    for g in range(groups):
        diag = jnp.sum(jnp.where(lane == sub + 8 * g, left[g], 0.0), axis=1, keepdims=True)
        out.append(right[g] * (1.0 / jnp.sqrt(diag)))
    return jnp.concatenate(out, axis=0)


def eliminate_blocks(x_ref, first, last):
    def block(b, carry):
        at = pl.multiple_of(b * TILE, TILE)
        inverse = inverse_factor(x_ref[pl.ds(at, TILE), pl.ds(at, TILE)])
        solved = jnp.dot(inverse, x_ref[pl.ds(at, TILE), :], precision=lax.Precision.HIGHEST, preferred_element_type=jnp.float32)
        lanes = lax.broadcasted_iota(jnp.int32, (TILE, PANEL), 1)

        @pl.when(b < PANEL // TILE - 1)
        def _():
            coef = jnp.where(lanes >= at + TILE, solved[:, :PANEL], 0.0)
            x_ref[...] -= jnp.dot(coef.T, solved, precision=lax.Precision.HIGHEST, preferred_element_type=jnp.float32)

        x_ref[pl.ds(at, TILE), :] = solved
        return carry

    lax.fori_loop(first, last, block, 0)


def front_kernel(sample_count, shift_ref, feat_panel_ref, feat_ref, moment_panel_ref, x_ref):
    width = feat_ref.shape[1]
    start = 2 * PANEL
    panel_t = feat_panel_ref[...].T
    dot = functools.partial(jnp.dot, preferred_element_type=jnp.float32)
    rows = lax.broadcasted_iota(jnp.int32, (PANEL, PANEL), 0)
    cols = lax.broadcasted_iota(jnp.int32, (PANEL, PANEL), 1)
    eye = jnp.where(rows == cols, 1.0, 0.0)
    x_ref[:, 0:PANEL] = dot(panel_t, feat_panel_ref[...]) / sample_count + ridge * eye
    x_ref[:, PANEL:start] = eye
    rows = lax.broadcasted_iota(jnp.int32, (PANEL, width), 0)
    cols = lax.broadcasted_iota(jnp.int32, (PANEL, width), 1)
    own = jnp.where(rows == cols + shift_ref[0], ridge, 0.0)
    x_ref[:, start : start + width] = dot(panel_t, feat_ref[...]) / sample_count + own
    column = jnp.sum(eye * (moment_panel_ref[...] / sample_count), axis=1, keepdims=True)
    x_ref[:, start + width :] = jnp.broadcast_to(column, (PANEL, LANES))
    eliminate_blocks(x_ref, 0, PANEL // TILE // 2)


def back_kernel(sample_count, x_in_ref, moment_ref, inv_high_ref, inv_low_ref, cross_high_ref, cross_low_ref, reduced_ref, x_ref):
    width = moment_ref.shape[1]
    start = 2 * PANEL
    x_ref[...] = x_in_ref[...]
    eliminate_blocks(x_ref, PANEL // TILE // 2, PANEL // TILE)
    inv_high_ref[...], inv_low_ref[...] = split(x_ref[:, PANEL:start].T)
    cross = x_ref[:, start : start + width]
    cross_high_ref[...], cross_low_ref[...] = split(cross)
    solved = x_ref[:, start + width : start + width + 1]
    reduced = moment_ref[...] / sample_count - jnp.sum(cross * solved, axis=0, keepdims=True)
    reduced_ref[...] = jnp.sqrt(jnp.float32(sample_count)) * reduced


def eliminate_front(shift, feat_panel, feat, moment_panel):
    count, width = feat.shape
    vmem = pl.BlockSpec(memory_space=pltpu.VMEM)
    return pl.pallas_call(
        functools.partial(front_kernel, count),
        in_specs=[pl.BlockSpec(memory_space=pltpu.SMEM)] + [vmem] * 3,
        out_specs=vmem,
        out_shape=jax.ShapeDtypeStruct((PANEL, 2 * PANEL + width + LANES), jnp.float32),
        cost_estimate=pl.CostEstimate(flops=20 * 10**9, bytes_accessed=8 * 10**6, transcendentals=0),
        compiler_params=pltpu.CompilerParams(vmem_limit_bytes=VMEM_BYTES),
    )(shift, feat_panel, feat, moment_panel)


def eliminate_back(count, state, moment):
    width = moment.shape[1]
    vmem = pl.BlockSpec(memory_space=pltpu.VMEM)
    square = jax.ShapeDtypeStruct((PANEL, PANEL), jnp.bfloat16)
    wide = jax.ShapeDtypeStruct((PANEL, width), jnp.bfloat16)
    return pl.pallas_call(
        functools.partial(back_kernel, count),
        in_specs=[vmem] * 2,
        out_specs=[vmem] * 5,
        out_shape=[square, square, wide, wide, jax.ShapeDtypeStruct((1, width), jnp.float32)],
        scratch_shapes=[pltpu.VMEM(state.shape, jnp.float32)],
        cost_estimate=pl.CostEstimate(flops=20 * 10**9, bytes_accessed=8 * 10**6, transcendentals=0),
        compiler_params=pltpu.CompilerParams(vmem_limit_bytes=VMEM_BYTES),
    )(state, moment)


def three_pass(left, right_high, right_low):
    high, low = split(left)
    dot = functools.partial(jnp.dot, preferred_element_type=jnp.float32)
    return dot(high, right_high) + (dot(high, right_low) + dot(low, right_high))


def main_kernel(
    sample_count,
    blocks,
    order_ref,
    place_ref,
    pos_ref,
    *refs,
):
    freq_refs = refs[:blocks]
    (
        emb_ref,
        treated_ref,
        feat_ref,
        feat_panel_ref,
        inv_high_ref,
        inv_low_ref,
        cross_high_ref,
        cross_low_ref,
        schur_ref,
        panel_ref,
        slots,
        sems,
    ) = refs[blocks:]
    now = pl.program_id(0)

    def fetch(index, slot):
        for k in range(blocks):

            @pl.when(index == k)
            def _():
                pltpu.make_async_copy(freq_refs[k], slots.at[slot], sems.at[slot]).start()

    @pl.when(now == 0)
    def _():
        fetch(0, 0)

    fetch(now + 1, lax.rem(now + 1, 2))
    slot = lax.rem(now, 2)
    pltpu.make_async_copy(freq_refs[0], slots.at[slot], sems.at[slot]).wait()

    height = slots.shape[1]
    count, emb_width = emb_ref.shape
    width = feat_ref.shape[1]
    parts = slots[slot, :, emb_width : emb_width + LANES].astype(jnp.float32)
    base = (parts[:, 0:1] + parts[:, 1:2]) + parts[:, 2:3]
    full = (parts[:, 3:4] + parts[:, 4:5]) + parts[:, 5:6]
    own = jnp.zeros((height, width), jnp.float32)
    panel = jnp.zeros((height, PANEL), jnp.float32)
    step = count // pos_ref.shape[0]
    for j in range(count // step):
        at = j * step
        emb = emb_ref[pl.ds(pl.multiple_of(pos_ref[j] * step, step), step), :]
        scaled = lax.dot_general(
            slots[slot, :, :emb_width], emb, (((1,), (1,)), ((), ())), preferred_element_type=jnp.float32
        )
        phase = jnp.where(treated_ref[:, at : at + step] > 0.5, full, base)
        features = cosine_turns(scaled * turn + phase).astype(jnp.bfloat16)
        own += jnp.dot(features, feat_ref[at : at + step, :], preferred_element_type=jnp.float32)
        panel += jnp.dot(features, feat_panel_ref[at : at + step, :], preferred_element_type=jnp.float32)
    first = place_ref[0] + order_ref[now] * height
    rows = first + lax.broadcasted_iota(jnp.int32, (height, width), 0)
    cols = place_ref[1] + lax.broadcasted_iota(jnp.int32, (height, width), 1)
    own = own / sample_count + jnp.where(rows == cols, ridge, 0.0)
    rows = first + lax.broadcasted_iota(jnp.int32, (height, PANEL), 0)
    cols = place_ref[2] + lax.broadcasted_iota(jnp.int32, (height, PANEL), 1)
    panel = panel / sample_count + jnp.where(rows == cols, ridge, 0.0)
    factor = three_pass(panel, inv_high_ref[...], inv_low_ref[...])
    panel_ref[...] = factor
    schur_ref[...] = own - three_pass(factor, cross_high_ref[...], cross_low_ref[...])


def main(order, place, pos, freqs, emb, treated, feat, feat_panel, solved):
    blocks = len(freqs)
    height = freqs[0].shape[0]
    row_height = blocks * height
    emb_width = emb.shape[1]
    count, width = feat.shape
    fixed = lambda array: pl.BlockSpec(array.shape, lambda i, *_: (0, 0), pipeline_mode=pl.Buffered(1))
    moved = lambda cols: pl.BlockSpec((height, cols), lambda i, order, *_: (order[i], 0))
    flops = 2 * row_height * (count * (emb_width + width + PANEL) + 3 * PANEL * (PANEL + width))
    return pl.pallas_call(
        functools.partial(main_kernel, count, blocks),
        grid_spec=pltpu.PrefetchScalarGridSpec(
            num_scalar_prefetch=3,
            grid=(blocks,),
            in_specs=[pl.BlockSpec(memory_space=pl.ANY)] * blocks
            + [fixed(array) for array in (emb, treated, feat, feat_panel, *solved)],
            out_specs=[moved(width), moved(PANEL)],
            scratch_shapes=[
                pltpu.VMEM((2, height, freqs[0].shape[1]), jnp.bfloat16),
                pltpu.SemaphoreType.DMA((2,)),
            ],
        ),
        out_shape=[
            jax.ShapeDtypeStruct((row_height, width), jnp.float32),
            jax.ShapeDtypeStruct((row_height, PANEL), jnp.float32),
        ],
        cost_estimate=pl.CostEstimate(flops=flops, bytes_accessed=30 * 10**6, transcendentals=count * row_height),
        compiler_params=pltpu.CompilerParams(vmem_limit_bytes=VMEM_BYTES),
    )(order, place, pos, *freqs, emb, treated, feat, feat_panel, *solved)


def swap(value, bits):
    return lax.ppermute(value, "feat", [(f, f ^ bits) for f in range(lax.axis_size("feat"))])


def gather_samples_staged(embeddings, marks, samp_index, feat_index):
    part = embeddings.shape[0] // 2
    core = feat_index % 2
    mine = lax.dynamic_slice_in_dim(embeddings, core * part, part, 0)
    got = lax.ppermute(mine, "samp", [(0, 1), (1, 0)])
    other_marks = lax.ppermute(marks, "samp", [(0, 1), (1, 0)])
    emb = jnp.concatenate([embeddings, got, swap(got, 1)], axis=0)
    piece = jnp.arange(4, dtype=jnp.int32)
    pos = jnp.where(piece // 2 == samp_index, piece % 2, jnp.where(piece % 2 == core, 2, 3))
    first = samp_index == 0
    marks = jnp.concatenate([jnp.where(first, marks, other_marks), jnp.where(first, other_marks, marks)], axis=1)
    return emb, marks, pos.astype(jnp.int32)


def per_device(embeddings, frequencies, phases, treat_freq, treatment, flips, panel):
    samp_size = lax.axis_size("samp")
    feat_size = lax.axis_size("feat")
    samp_index = lax.axis_index("samp")
    feat_index = lax.axis_index("feat")
    emb_width, col_width = frequencies.shape
    feat_total = col_width * feat_size
    row_height = feat_total // samp_size
    first_col = panel[0] * PANEL
    first_dev = first_col // col_width
    staged = samp_size == 2 and feat_size == 16
    half = 8

    base = phases * turn
    parts = jnp.stack(thirds(base) + thirds(base + treat_freq * turn))
    freq = jnp.concatenate([frequencies, jnp.pad(parts, ((0, 10), (0, 0)))], axis=0)
    freq_t = jnp.concatenate([frequencies.T, jnp.pad(parts.T, ((0, 0), (0, LANES - 6)))], axis=1)

    treated = treatment.astype(jnp.float32)
    flipped = flips.astype(jnp.float32)
    counter = treated + flipped - 2.0 * treated * flipped
    marks = jnp.stack([treated, counter])
    if staged:
        emb, marks, pos = gather_samples_staged(embeddings, marks, samp_index, feat_index)
        mates = [(s * 16 + f, s * 16 + (f ^ half)) for s in range(2) for f in range(s * half, (s + 1) * half)]
        crossed = lax.ppermute(freq_t, ("samp", "feat"), mates)
        mine = jnp.where(feat_index // half == samp_index, freq_t, crossed)
    else:
        emb = lax.all_gather(embeddings, "samp", axis=0, tiled=True)
        marks = lax.all_gather(marks, "samp", axis=1, tiled=True)
        pos = jnp.arange(emb.shape[0] // 512, dtype=jnp.int32)

    panel_freq = []
    for member in range(PANEL // col_width):
        own = feat_index == first_dev + member
        panel_freq.append(lax.psum(jnp.where(own, freq, jnp.zeros_like(freq)), "feat"))
    panel_freq = jnp.concatenate(panel_freq, axis=1)

    treated_col, counter_col = marks[0][:, None], marks[1][:, None]
    feat, moment = make_features(pos, emb, freq, treated_col, counter_col)
    if staged:
        mine, panel_freq, feat = lax.optimization_barrier((mine, panel_freq, feat))
        near = [swap(mine, 4), swap(mine, 2), swap(mine, 6)]
    feat_panel, moment_panel = make_features(pos, emb, panel_freq, treated_col, counter_col)
    own_col = feat_index * col_width
    shift = (own_col - first_col).reshape(1).astype(jnp.int32)
    state = eliminate_front(shift, feat_panel, feat, moment_panel)
    if staged:
        state, near = lax.optimization_barrier((state, near))
        near = [mine] + near
        freqs = near + [swap(block, 1) for block in near]
        order = jnp.bitwise_xor(feat_index % half, jnp.array([0, 4, 2, 6, 1, 5, 3, 7], jnp.int32))
    else:
        rows = lax.all_gather(freq_t, "feat", axis=0, tiled=True)
        rows = lax.dynamic_slice_in_dim(rows, samp_index * row_height, row_height, 0)
        freqs = jnp.split(rows, row_height // col_width, axis=0)
        order = jnp.arange(row_height // col_width, dtype=jnp.int32)
    *solved, reduced = eliminate_back(emb.shape[0], state, moment)
    place = jnp.stack([samp_index * row_height, own_col, first_col]).astype(jnp.int32)
    schur, panel_factor = main(order, place, pos, freqs, emb, marks[:1], feat, feat_panel, solved)
    return schur, panel_factor, reduced[0]


def solution(mesh):
    return jax.shard_map(
        per_device,
        mesh=mesh,
        in_specs=(
            P("samp", None),
            P(None, "feat"),
            P("feat"),
            P("feat"),
            P("samp"),
            P("samp"),
            P(),
        ),
        out_specs=(P("samp", "feat"), P("samp", None), P("feat")),
        check_vma=False,
    )
```

time: 330 us -> 300 us (0.909)
  waiting for transfers between devices: 40 us -> 111 us
  blocking collectives: 40.4 us -> 0 us
  starting transfers between devices: 33.3 us -> 13.3 us
  local copies, waits for them, and re-layouts: 30.4 us -> 12 us
  Pallas kernels: 150 us -> 141 us
  matrix products: 6.86 us -> 0 us
  other arithmetic: 12.5 us -> 7.62 us
    psum x1, waiting for transfers between devices: 15.5 us -> 83.1 us  [per_device(): lax.psum(jnp.where(own, freq, jnp.zeros_like(freq)), 'feat')]
    all_gather x1 -> x0, blocking collectives: 40.4 us -> none  [per_device(): lax.all_gather(jnp.stack([base_own, base_own + treat_freq * turn]), 'feat...]
    ppermute x9, starting transfers between devices: 30.3 us -> 10.2 us  [the longest x1 6.05 us: per_device(): crossed = lax.ppermute(freq_t, ('samp', 'feat'), mates)]
    ppermute x1, waiting for transfers between devices: 0.01 us -> 9.93 us  [gather_samples_staged(): got = lax.ppermute(mine, 'samp', [(0, 1), (1, 0)])]
    unnamed x22 -> x25, local copies, waits for them, and re-layouts: 14.4 us -> 5.37 us
    pallas_call x4 -> x5, Pallas kernels: 150 us -> 141 us  [the longest x1 67.7 us: main(): pl.pallas_call(functools.partial(main_kernel, count, blocks), grid_spec=p...]
    ppermute x9, waiting for transfers between devices: 24.5 us -> 17.5 us  [the longest x8 11.8 us: swap(): lax.ppermute(value, 'feat', [(f, f ^ bits) for f in range(lax.axis_size('...]
    dot_general x2 -> x0, matrix products: 6.86 us -> none  [per_device(): lax.dot_general(left, right, (((0,), (0,)), ((), ())), preferred_element_...]
  transfers between devices with their start and end apart: 12 -> 12, of which waited for: 3 -> 4; matrix products, arithmetic and copies ran while one was open for 14% -> 6% of each run, Pallas kernels for 25% -> 25%
where the time goes in v2:
time: 300 us
  Pallas kernels  141 us (47%)
  waiting for transfers between devices  111 us (37%)
  between operations  14.9 us (5%)
  starting transfers between devices  13.3 us (4%)
  local copies, waits for them, and re-layouts  12 us (4%)
  other arithmetic  7.62 us (3%)
    psum x1, waiting for transfers between devices, per_device(): lax.psum(jnp.where(own, freq, jnp.zeros_like(freq)), 'feat')  83.1 us
    pallas_call x1, Pallas kernels, main(): pl.pallas_call(functools.partial(main_kernel, count, blocks), grid_spec=p...  67.7 us
    pallas_call x1, Pallas kernels, eliminate_front(): pl.pallas_call(functools.partial(front_kernel, count), in_specs=[pl.Block...  27.5 us
    pallas_call x2, Pallas kernels, make_features(): pl.pallas_call(feature_kernel, grid_spec=pltpu.PrefetchScalarGridSpec(num...  23.7 us
    pallas_call x1, Pallas kernels, eliminate_back(): pl.pallas_call(functools.partial(back_kernel, count), in_specs=[vmem] * 2...  22.5 us
    ppermute x8, waiting for transfers between devices, swap(): lax.ppermute(value, 'feat', [(f, f ^ bits) for f in range(lax.axis_size('...  11.8 us
    ppermute x1, waiting for transfers between devices, gather_samples_staged(): got = lax.ppermute(mine, 'samp', [(0, 1), (1, 0)])  9.93 us
    ppermute x1, starting transfers between devices, per_device(): crossed = lax.ppermute(freq_t, ('samp', 'feat'), mates)  6.05 us
  transfers between devices with their start and end apart: 12, of which 4 were waited for; matrix products, arithmetic and copies ran while one was open for 6% of the time, Pallas kernels for 25%

profile of v2, /device:TPU:0, one launch (start us, length us, event | category | flops | bytes accessed | tf_op | source)
XLA Modules:
  0.0 299.7 jit_solution(6352571401126134538)
XLA Ops:
  7.2 0.8 convert_element_type.34
  8.0 0.7 multiply_subtract_fusion
  8.7 3.0 %collective-permute-start.3 = (f32[2,1024]{1,0:T(2,128)S(1)}, f32[2,1024]{1,0:T(2,128)S(1)}, u32[]{:S(2)}, u32[]{:S(2)}) collective-permute-start(f32[2,1024]{1,0:T(2,128)S(1)} %pad_maximum_fusion.1), channel_id=1, source_target_pairs={{0,16},{16,0},{1,17},{17,1},{2,18},{18,2},{3,19},{19,3},{4,20},{20... | collective-permute-start | bytes 24584 | tf_op jit(solution)/shard_map/ppermute | solution.py:337
  11.7 2.4 constant_dynamic-slice_fusion
  14.3 0.2 copy.26
  14.5 0.5 copy.25
  15.0 1.1 fusion.2
  16.1 6.0 %collective-permute-start = (bf16[512,1152]{1,0:T(8,128)(2,1)}, bf16[512,1152]{1,0:T(8,128)(2,1)}, u32[]{:S(2)}, u32[]{:S(2)}) collective-permute-start(bf16[512,1152]{1,0:T(8,128)(2,1)} %fusion.2), channel_id=1, source_target_pairs={{0,8},{1,9},{2,10},{3,11},{4,12},{5,13},{6,14},{7,15},{24,16},{25,... | collective-permute-start | bytes 3538952 | tf_op jit(solution)/shard_map/ppermute | solution.py:371
  22.9 3.0 fusion.3
  25.9 0.6 compare_select_fusion.1.pos_ref
  26.5 1.5 constant_dynamic-update-slice_fusion.2
  28.0 0.5 broadcast_xor_fusion.order_ref
  28.5 0.6 pad_add_fusion.place_ref
  29.1 9.9 %collective-permute-done.1 = bf16[512,1024]{1,0:T(8,128)(2,1)} collective-permute-done((bf16[512,1024]{1,0:T(8,128)(2,1)}, bf16[512,1024]{1,0:T(8,128)(2,1)}, u32[]{:S(2)}, u32[]{:S(2)}) %collective-permute-start.1) | collective-permute-done | bytes 1048608 | tf_op jit(solution)/shard_map/ppermute | solution.py:336
  39.1 1.3 copy.28.counter_ref
  40.4 1.4 copy.27.treated_ref
  41.8 2.3 constant_dynamic-update-slice_fusion.1
  44.1 5.7 %collective-permute-done = bf16[512,1152]{1,0:T(8,128)(2,1)} collective-permute-done((bf16[512,1152]{1,0:T(8,128)(2,1)}, bf16[512,1152]{1,0:T(8,128)(2,1)}, u32[]{:S(2)}, u32[]{:S(2)}) %collective-permute-start) | collective-permute-done | bytes 1179680 | tf_op jit(solution)/shard_map/ppermute | solution.py:371
  49.8 0.3 broadcast_select_fusion.refs_0_
  50.1 1.2 constant_dynamic-update-slice_fusion.emb_ref.refs_8_
  51.4 11.9 %shard_map.103 = (bf16[2048,512]{1,0:T(8,128)(2,1)}, f32[1,512]{1,0:T(1,128)}) custom-call(s32[4]{0:T(128)} %compare_select_fusion.1.pos_ref, bf16[2048,1024]{1,0:T(8,128)(2,1)} %constant_dynamic-update-slice_fusion.emb_ref.refs_8_, bf16[1040,512]{1,0:T(8,128)(2,1)} %get-tuple-element.39.freq_ref, f32[2048,1]{1,0:T(8,128)} %copy.27.treated_ref, ...), custom_call_target="tpu_custom_call" | custom-call | flops 2147483648 | bytes 4194304 | tf_op jit(solution)/shard_map/pallas_call | solution.py:65
  63.3 83.1 %all-reduce.4.cloned.1.call-done.freq_ref = bf16[1040,512]{1,0:T(8,128)(2,1)} async-done(((bf16[1040,512]{1,0:T(8,128)(2,1)}), bf16[1040,512]{1,0:T(8,128)(2,1)}) %all-reduce.4.cloned.1.call-update) | async-done | bytes 1064976 | tf_op jit(solution)/shard_map/psum | solution.py:381
  146.4 1.6 collective-permute-start.6
  148.0 1.4 collective-permute-start.5
  149.5 0.5 collective-permute-start.4
  149.9 11.8 %shard_map.104 = (bf16[2048,512]{1,0:T(8,128)(2,1)}, f32[1,512]{1,0:T(1,128)}) custom-call(s32[4]{0:T(128)} %compare_select_fusion.1.pos_ref, bf16[2048,1024]{1,0:T(8,128)(2,1)} %constant_dynamic-update-slice_fusion.emb_ref.refs_8_, bf16[1040,512]{1,0:T(8,128)(2,1)} %all-reduce.4.cloned.1.call-done.freq_ref, f32[2048,1]{1,0:T(8,128)} %copy.27.treated_ref, ...), custom_call_target="tpu_custom_call" | custom-call | flops 2147483648 | bytes 4194304 | tf_op jit(solution)/shard_map/pallas_call | solution.py:65
  161.7 27.5 %shard_map.105.x_in_ref = f32[512,1664]{1,0:T(8,128)} custom-call(s32[1]{0:T(128)} %bitcast.9.shift_ref, bf16[2048,512]{1,0:T(8,128)(2,1)} %get-tuple-element.24.feat_panel_ref.refs_11_, bf16[2048,512]{1,0:T(8,128)(2,1)} %get-tuple-element.25.feat_ref.refs_10_, f32[1,512]{1,0:T(1,128)} %get-tuple-element.26.moment_panel_ref), custom_call_target="tpu_custom_call" | custom-call | flops 20000000000 | bytes 8000000 | tf_op jit(solution)/shard_map/pallas_call | solution.py:194
  189.2 11.8 %collective-permute-done.5.refs_2_ = bf16[512,1152]{1,0:T(8,128)(2,1)S(1)} collective-permute-done((bf16[512,1152]{1,0:T(8,128)(2,1)S(1)}, bf16[512,1152]{1,0:T(8,128)(2,1)S(1)}, u32[]{:S(2)}, u32[]{:S(2)}) %collective-permute-start.5) | collective-permute-done | bytes 1179680 | tf_op jit(solution)/shard_map/ppermute | solution.py:329
  201.1 0.5 collective-permute-start.9
  201.7 22.5 %shard_map.106 = (bf16[512,512]{1,0:T(8,128)(2,1)}, bf16[512,512]{1,0:T(8,128)(2,1)}, bf16[512,512]{1,0:T(8,128)(2,1)}, bf16[512,512]{1,0:T(8,128)(2,1)}, f32[1,512]{1,0:T(1,128)}) custom-call(f32[512,1664]{1,0:T(8,128)} %shard_map.105.x_in_ref, f32[1,512]{1,0:T(1,128)} %get-tuple-element.31.moment_ref), custom_call_target="tpu_custom_call" | custom-call | flops 20000000000 | bytes 8000000 | tf_op jit(solution)/shard_map/pallas_call | solution.py:209
  224.2 1.0 copy-done.6
  225.2 67.7 %shard_map.107 = (f32[4096,512]{1,0:T(8,128)}, f32[4096,512]{1,0:T(8,128)}) custom-call(s32[8]{0:T(128)} %broadcast_xor_fusion.order_ref, s32[3]{0:T(128)} %pad_add_fusion.place_ref, s32[4]{0:T(128)} %compare_select_fusion.1.pos_ref, bf16[512,1152]{1,0:T(8,128)(2,1)} %copy-done.2, bf16[512,1152]{1,0:T(8,128)(2,1)} %copy-done.9, bf16[512,1152]{1,0:T(8,128)(2,1)} %copy-done.8, ...), custom_call_target="tpu_custom_call" | custom-call | flops 47244640256 | bytes 30000000 | tf_op jit(solution)/shard_map/pallas_call | solution.py:306
  (47 shorter events, 0.5 us)
Async XLA Ops:
  7.2 7.0 %copy-start.4 = (f32[512]{0:T(512)S(1)}, f32[512]{0:T(512)}, u32[]{:S(2)}) copy-start(f32[512]{0:T(512)} %param.11) | copy-start | bytes 6148
  7.2 7.0 %copy-start.5 = (f32[512]{0:T(512)S(1)}, f32[512]{0:T(512)}, u32[]{:S(2)}) copy-start(f32[512]{0:T(512)} %param.10) | copy-start | bytes 6148
  7.2 7.3 %copy-start.1 = (bf16[1024,512]{1,0:T(8,128)(2,1)S(1)}, bf16[1024,512]{1,0:T(8,128)(2,1)}, u32[]{:S(2)}) copy-start(bf16[1024,512]{1,0:T(8,128)(2,1)} %param.9) | copy-start | bytes 3145732
  7.2 139.2 %all-reduce.4.cloned.1.call-start = ((), (), s32[]{:S(2)}) async-start(), calls=%async_computation | async-start | bytes 2129920 | tf_op jit(solution)/shard_map/psum | solution.py:381
  8.7 30.3 %collective-permute-start.3 = (f32[2,1024]{1,0:T(2,128)S(1)}, f32[2,1024]{1,0:T(2,128)S(1)}, u32[]{:S(2)}, u32[]{:S(2)}) collective-permute-start(f32[2,1024]{1,0:T(2,128)S(1)} %pad_maximum_fusion.1), channel_id=1, source_target_pairs={{0,16},{16,0},{1,17},{17,1},{2,18},{18,2},{3,19},{19,3},{4,20},{20... | collective-permute-start | bytes 24584 | tf_op jit(solution)/shard_map/ppermute | solution.py:337
  14.1 24.9 %collective-permute-start.1 = (bf16[512,1024]{1,0:T(8,128)(2,1)}, bf16[512,1024]{1,0:T(8,128)(2,1)}, u32[]{:S(2)}, u32[]{:S(2)}) collective-permute-start(bf16[512,1024]{1,0:T(8,128)(2,1)} %constant_dynamic-slice_fusion), channel_id=1, source_target_pairs={{0,16},{16,0},{1,17},{17,1},{2,18},{18,2},{3,19},{19,3},{4,20},{20... | collective-permute-start | bytes 3145736 | tf_op jit(solution)/shard_map/ppermute | solution.py:336
  16.1 33.7 %collective-permute-start = (bf16[512,1152]{1,0:T(8,128)(2,1)}, bf16[512,1152]{1,0:T(8,128)(2,1)}, u32[]{:S(2)}, u32[]{:S(2)}) collective-permute-start(bf16[512,1152]{1,0:T(8,128)(2,1)} %fusion.2), channel_id=1, source_target_pairs={{0,8},{1,9},{2,10},{3,11},{4,12},{5,13},{6,14},{7,15},{24,16},{25,... | collective-permute-start | bytes 3538952 | tf_op jit(solution)/shard_map/ppermute | solution.py:371
  22.8 3.6 %copy-start = (bf16[1024,1024]{1,0:T(8,128)(2,1)S(1)}, bf16[1024,1024]{1,0:T(8,128)(2,1)}, u32[]{:S(2)}) copy-start(bf16[1024,1024]{1,0:T(8,128)(2,1)} %param.8) | copy-start | bytes 6291460
  26.5 1.5 copy-start.10
  39.0 11.1 %collective-permute-start.2 = (bf16[512,1024]{1,0:T(8,128)(2,1)}, bf16[512,1024]{1,0:T(8,128)(2,1)S(1)}, u32[]{:S(2)}, u32[]{:S(2)}) collective-permute-start(bf16[512,1024]{1,0:T(8,128)(2,1)} %collective-permute-done.1), channel_id=1, source_target_pairs={{0,1},{1,0},{2,3},{3,2},{4,5},{5,4},{6,7},{7,6},{8,9},{9,8},{10,11... | collective-permute-start | bytes 3145736 | tf_op jit(solution)/shard_map/ppermute | solution.py:329
  39.1 5.0 %copy-start.3 = (f32[1,2048]{1,0:T(1,128)}, f32[1,2048]{1,0:T(1,128)S(1)}, u32[]{:S(2)}) copy-start(f32[1,2048]{1,0:T(1,128)S(1)} %get-tuple-element.42.refs_9_) | copy-start | bytes 24580
  50.1 99.4 %copy-start.2 = (bf16[512,1152]{1,0:T(8,128)(2,1)}, bf16[512,1152]{1,0:T(8,128)(2,1)S(1)}, u32[]{:S(2)}) copy-start(bf16[512,1152]{1,0:T(8,128)(2,1)S(1)} %broadcast_select_fusion.refs_0_) | copy-start | bytes 3538948
  146.4 77.7 %collective-permute-start.7 = (bf16[512,1152]{1,0:T(8,128)(2,1)S(1)}, bf16[512,1152]{1,0:T(8,128)(2,1)S(1)}, u32[]{:S(2)}, u32[]{:S(2)}) collective-permute-start(bf16[512,1152]{1,0:T(8,128)(2,1)S(1)} %broadcast_select_fusion.refs_0_), channel_id=1, source_target_pairs={{0,1},{1,0},{2,3},{3,2},{4,5},{5,4},{6,7},{7,6},{8,9},{9,8},{10,11... | collective-permute-start | bytes 3538952 | tf_op jit(solution)/shard_map/ppermute | solution.py:329
  146.4 42.8 %collective-permute-start.6 = (bf16[512,1152]{1,0:T(8,128)(2,1)S(1)}, bf16[512,1152]{1,0:T(8,128)(2,1)S(1)}, u32[]{:S(2)}, u32[]{:S(2)}) collective-permute-start(bf16[512,1152]{1,0:T(8,128)(2,1)S(1)} %broadcast_select_fusion.refs_0_), channel_id=1, source_target_pairs={{0,6},{1,7},{2,4},{3,5},{4,2},{5,3},{6,0},{7,1},{8,14},{9,15},{10,... | collective-permute-start | bytes 3538952 | tf_op jit(solution)/shard_map/ppermute | solution.py:329
  148.0 53.0 %collective-permute-start.5 = (bf16[512,1152]{1,0:T(8,128)(2,1)S(1)}, bf16[512,1152]{1,0:T(8,128)(2,1)S(1)}, u32[]{:S(2)}, u32[]{:S(2)}) collective-permute-start(bf16[512,1152]{1,0:T(8,128)(2,1)S(1)} %broadcast_select_fusion.refs_0_), channel_id=1, source_target_pairs={{0,2},{1,3},{2,0},{3,1},{4,6},{5,7},{6,4},{7,5},{8,10},{9,11},{10,... | collective-permute-start | bytes 3538952 | tf_op jit(solution)/shard_map/ppermute | solution.py:329
  149.5 51.5 %collective-permute-start.4 = (bf16[512,1152]{1,0:T(8,128)(2,1)S(1)}, bf16[512,1152]{1,0:T(8,128)(2,1)S(1)}, u32[]{:S(2)}, u32[]{:S(2)}) collective-permute-start(bf16[512,1152]{1,0:T(8,128)(2,1)S(1)} %broadcast_select_fusion.refs_0_), channel_id=1, source_target_pairs={{0,4},{1,5},{2,6},{3,7},{4,0},{5,1},{6,2},{7,3},{8,12},{9,13},{10,... | collective-permute-start | bytes 3538952 | tf_op jit(solution)/shard_map/ppermute | solution.py:329
  189.2 34.9 %copy-start.7 = (bf16[512,1152]{1,0:T(8,128)(2,1)}, bf16[512,1152]{1,0:T(8,128)(2,1)S(1)}, u32[]{:S(2)}) copy-start(bf16[512,1152]{1,0:T(8,128)(2,1)S(1)} %collective-permute-done.6.refs_3_) | copy-start | bytes 3538948
  201.0 23.1 %copy-start.8 = (bf16[512,1152]{1,0:T(8,128)(2,1)}, bf16[512,1152]{1,0:T(8,128)(2,1)S(1)}, u32[]{:S(2)}) copy-start(bf16[512,1152]{1,0:T(8,128)(2,1)S(1)} %collective-permute-done.5.refs_2_) | copy-start | bytes 3538948
  201.0 23.1 %copy-start.9 = (bf16[512,1152]{1,0:T(8,128)(2,1)}, bf16[512,1152]{1,0:T(8,128)(2,1)S(1)}, u32[]{:S(2)}) copy-start(bf16[512,1152]{1,0:T(8,128)(2,1)S(1)} %collective-permute-done.4.refs_1_) | copy-start | bytes 3538948
  201.0 23.1 %collective-permute-start.8 = (bf16[512,1152]{1,0:T(8,128)(2,1)S(1)}, bf16[512,1152]{1,0:T(8,128)(2,1)}, u32[]{:S(2)}, u32[]{:S(2)}) collective-permute-start(bf16[512,1152]{1,0:T(8,128)(2,1)S(1)} %collective-permute-done.4.refs_1_), channel_id=1, source_target_pairs={{0,1},{1,0},{2,3},{3,2},{4,5},{5,4},{6,7},{7,6},{8,9},{9,8},{10,11... | collective-permute-start | bytes 3538952 | tf_op jit(solution)/shard_map/ppermute | solution.py:329
  201.1 23.0 %collective-permute-start.9 = (bf16[512,1152]{1,0:T(8,128)(2,1)S(1)}, bf16[512,1152]{1,0:T(8,128)(2,1)}, u32[]{:S(2)}, u32[]{:S(2)}) collective-permute-start(bf16[512,1152]{1,0:T(8,128)(2,1)S(1)} %collective-permute-done.5.refs_2_), channel_id=1, source_target_pairs={{0,1},{1,0},{2,3},{3,2},{4,5},{5,4},{6,7},{7,6},{8,9},{9,8},{10,11... | collective-permute-start | bytes 3538952 | tf_op jit(solution)/shard_map/ppermute | solution.py:329
  201.6 22.6 %collective-permute-start.10 = (bf16[512,1152]{1,0:T(8,128)(2,1)S(1)}, bf16[512,1152]{1,0:T(8,128)(2,1)}, u32[]{:S(2)}, u32[]{:S(2)}) collective-permute-start(bf16[512,1152]{1,0:T(8,128)(2,1)S(1)} %collective-permute-done.6.refs_3_), channel_id=1, source_target_pairs={{0,1},{1,0},{2,3},{3,2},{4,5},{5,4},{6,7},{7,6},{8,9},{9,8},{10,11... | collective-permute-start | bytes 3538952 | tf_op jit(solution)/shard_map/ppermute | solution.py:329
  224.1 1.0 copy-start.6
Sparse Core Ops, SparseCore 0:
  26.0 120.4 all-reduce.3

commit v3 on v2

--- a/solution.py
+++ b/solution.py
@@ -46,10 +46,12 @@
         moment_ref[...] = jnp.zeros_like(moment_ref)
 
     width = emb_ref.shape[1]
-    parts = [freq_ref[width + k : width + k + 1, :].astype(jnp.float32) for k in range(6)]
-    base = (parts[0] + parts[1]) + parts[2]
-    full = (parts[3] + parts[4]) + parts[5]
-    scaled = jnp.dot(emb_ref[...], freq_ref[:width, :], preferred_element_type=jnp.float32) * turn
+    parts = freq_ref[:, width:].astype(jnp.float32).T
+    base = (parts[0:1] + parts[1:2]) + parts[2:3]
+    full = (parts[3:4] + parts[4:5]) + parts[5:6]
+    scaled = lax.dot_general(
+        emb_ref[...], freq_ref[:, :width], (((1,), (1,)), ((), ())), preferred_element_type=jnp.float32
+    ) * turn
     observed = cosine_turns(scaled + jnp.where(treated_ref[...] > 0.5, full, base))
     counterfactual = cosine_turns(scaled + jnp.where(counter_ref[...] > 0.5, full, base))
     feat_ref[...] = observed.astype(jnp.bfloat16)
@@ -58,7 +60,7 @@
 
 def make_features(pos, emb, freq, treated, counter):
     count, emb_width = emb.shape
-    rows, width = freq.shape
+    width = freq.shape[0]
     step = 256
     ratio = count // pos.shape[0] // step
     whole = lambda shape: pl.BlockSpec(shape, lambda i, pos: (0, 0))
@@ -69,7 +71,7 @@
             grid=(count // step,),
             in_specs=[
                 pl.BlockSpec((step, emb_width), lambda i, pos: (pos[i // ratio] * ratio + i % ratio, 0)),
-                whole((rows, width)),
+                whole(freq.shape),
                 pl.BlockSpec((step, 1), lambda i, pos: (i, 0)),
                 pl.BlockSpec((step, 1), lambda i, pos: (i, 0)),
             ],
@@ -325,6 +327,77 @@
     )(order, place, pos, *freqs, emb, treated, feat, feat_panel, *solved)
 
 
+def spread_kernel(axis_size, x_ref, out_ref, sums, arrived, send_sems, recv_sems):
+    samp, feat = lax.axis_index("samp"), lax.axis_index("feat")
+    rows = x_ref.shape[0]
+    bits = []
+    while (1 << len(bits)) < axis_size:
+        bits.append(1 << len(bits))
+    sides = [(feat // bit) % 2 for bit in bits]
+    mates = [feat + bit * (1 - 2 * side) for bit, side in zip(bits, sides)]
+
+    barrier = pltpu.get_barrier_semaphore()
+    for mate in mates:
+        pl.semaphore_signal(barrier, inc=1, device_id=(samp, mate), device_id_type=pl.DeviceIdType.MESH)
+    pl.semaphore_wait(barrier, len(bits))
+
+    def send(source, target, mate, index):
+        copy = pltpu.make_async_remote_copy(
+            src_ref=source,
+            dst_ref=target,
+            send_sem=send_sems.at[index],
+            recv_sem=recv_sems.at[index],
+            device_id=(samp, mate),
+            device_id_type=pl.DeviceIdType.MESH,
+        )
+        copy.start()
+        copy.wait()
+
+    first = 0
+    firsts = []
+    size = rows
+    source = x_ref
+    landing = 0
+    for index, (side, mate) in enumerate(zip(sides, mates)):
+        size //= 2
+        kept = pl.multiple_of(first + side * size, 16)
+        given = pl.multiple_of(first + (1 - side) * size, 16)
+        place = pl.ds(landing, size)
+        send(source.at[pl.ds(given, size)], arrived.at[place], mate, index)
+        total = source[pl.ds(kept, size), :] + arrived[place, :]
+        landing += size
+        first = kept
+        firsts.append((first, size))
+        if index < len(bits) - 1:
+            sums[pl.ds(kept, size), :] = total
+            source = sums
+        else:
+            out_ref[pl.ds(kept, size), :] = total
+    for index in reversed(range(len(bits))):
+        first, size = firsts[index]
+        part = out_ref.at[pl.ds(first, size)]
+        send(part, part, mates[index], len(bits) + index)
+
+
+def spread(x):
+    axis_size = lax.axis_size("feat")
+    steps = 2 * (axis_size.bit_length() - 1)
+    return pl.pallas_call(
+        functools.partial(spread_kernel, axis_size),
+        in_specs=[pl.BlockSpec(memory_space=pltpu.VMEM)],
+        out_specs=pl.BlockSpec(memory_space=pltpu.VMEM),
+        out_shape=jax.ShapeDtypeStruct(x.shape, x.dtype),
+        scratch_shapes=[
+            pltpu.VMEM(x.shape, x.dtype),
+            pltpu.VMEM(x.shape, x.dtype),
+            pltpu.SemaphoreType.DMA((steps,)),
+            pltpu.SemaphoreType.DMA((steps,)),
+        ],
+        cost_estimate=pl.CostEstimate(flops=45 * 10**9, bytes_accessed=2 * 10**6, transcendentals=0),
+        compiler_params=pltpu.CompilerParams(collective_id=0, has_side_effects=True, vmem_limit_bytes=16 * 1024 * 1024),
+    )(x)
+
+
 def swap(value, bits):
     return lax.ppermute(value, "feat", [(f, f ^ bits) for f in range(lax.axis_size("feat"))])
 
@@ -353,12 +426,11 @@
     row_height = feat_total // samp_size
     first_col = panel[0] * PANEL
     first_dev = first_col // col_width
-    staged = samp_size == 2 and feat_size == 16
+    staged = samp_size == 2 and feat_size == 16 and col_width == PANEL
     half = 8
 
     base = phases * turn
     parts = jnp.stack(thirds(base) + thirds(base + treat_freq * turn))
-    freq = jnp.concatenate([frequencies, jnp.pad(parts, ((0, 10), (0, 0)))], axis=0)
     freq_t = jnp.concatenate([frequencies.T, jnp.pad(parts.T, ((0, 0), (0, LANES - 6)))], axis=1)
 
     treated = treatment.astype(jnp.float32)
@@ -375,14 +447,17 @@
         marks = lax.all_gather(marks, "samp", axis=1, tiled=True)
         pos = jnp.arange(emb.shape[0] // 512, dtype=jnp.int32)
 
-    panel_freq = []
-    for member in range(PANEL // col_width):
-        own = feat_index == first_dev + member
-        panel_freq.append(lax.psum(jnp.where(own, freq, jnp.zeros_like(freq)), "feat"))
-    panel_freq = jnp.concatenate(panel_freq, axis=1)
+    if staged:
+        panel_freq = spread(jnp.where(feat_index == first_dev, freq_t, jnp.zeros_like(freq_t)))
+    else:
+        panel_freq = []
+        for member in range(PANEL // col_width):
+            own = feat_index == first_dev + member
+            panel_freq.append(lax.psum(jnp.where(own, freq_t, jnp.zeros_like(freq_t)), "feat"))
+        panel_freq = jnp.concatenate(panel_freq, axis=0)
 
     treated_col, counter_col = marks[0][:, None], marks[1][:, None]
-    feat, moment = make_features(pos, emb, freq, treated_col, counter_col)
+    feat, moment = make_features(pos, emb, freq_t, treated_col, counter_col)
     if staged:
         mine, panel_freq, feat = lax.optimization_barrier((mine, panel_freq, feat))
         near = [swap(mine, 4), swap(mine, 2), swap(mine, 6)]

time: 300 us -> 267 us (0.89)
  waiting for transfers between devices: 111 us -> 25.9 us
  Pallas kernels: 141 us -> 206 us
  between operations: 14.9 us -> 1.69 us
    psum x1 -> x0, waiting for transfers between devices: 83.1 us -> none  [per_device(): lax.psum(jnp.where(own, freq, jnp.zeros_like(freq)), 'feat')]
    pallas_call x0 -> x1, Pallas kernels: none -> 64.7 us  [spread(): pl.pallas_call(functools.partial(spread_kernel, axis_size), in_specs=[pl....]
  transfers between devices with their start and end apart: 12 -> 11, of which waited for: 4 -> 3; matrix products, arithmetic and copies ran while one was open for 6% -> 5% of each run, Pallas kernels for 25% -> 48%
where the time goes in v3:
time: 267 us; the launch traced here: 266 us
  Pallas kernels  206 us (77%)
  waiting for transfers between devices  25.9 us (10%)
  starting transfers between devices  13.9 us (5%)
  local copies, waits for them, and re-layouts  13.7 us (5%)
  other arithmetic  4.69 us (2%)
    pallas_call x1, Pallas kernels, main(): pl.pallas_call(functools.partial(main_kernel, count, blocks), grid_spec=p...  67.7 us
    pallas_call x1, Pallas kernels, spread(): pl.pallas_call(functools.partial(spread_kernel, axis_size), in_specs=[pl....  64.7 us
    pallas_call x1, Pallas kernels, eliminate_front(): pl.pallas_call(functools.partial(front_kernel, count), in_specs=[pl.Block...  27.5 us
    pallas_call x2, Pallas kernels, make_features(): pl.pallas_call(feature_kernel, grid_spec=pltpu.PrefetchScalarGridSpec(num...  24.1 us
    pallas_call x1, Pallas kernels, eliminate_back(): pl.pallas_call(functools.partial(back_kernel, count), in_specs=[vmem] * 2...  22.5 us
    ppermute x8, waiting for transfers between devices, swap(): lax.ppermute(value, 'feat', [(f, f ^ bits) for f in range(lax.axis_size('...  10.9 us
    ppermute x1, waiting for transfers between devices, gather_samples_staged(): got = lax.ppermute(mine, 'samp', [(0, 1), (1, 0)])  9.12 us
    unnamed x25, local copies, waits for them, and re-layouts  7.47 us
  transfers between devices with their start and end apart: 11, of which 3 were waited for; matrix products, arithmetic and copies ran while one was open for 5% of the time, Pallas kernels for 48%

profile of v3, /device:TPU:0, one launch (start us, length us, event | category | flops | bytes accessed | tf_op | source)
XLA Modules:
  0.0 266.4 jit_solution(8213475681178612950)
XLA Ops:
  0.7 0.7 convert_element_type.32
  1.4 0.7 multiply_subtract_fusion
  2.1 3.0 %collective-permute-start.3 = (f32[2,1024]{1,0:T(2,128)S(1)}, f32[2,1024]{1,0:T(2,128)S(1)}, u32[]{:S(2)}, u32[]{:S(2)}) collective-permute-start(f32[2,1024]{1,0:T(2,128)S(1)} %pad_maximum_fusion.1), channel_id=1, source_target_pairs={{0,16},{16,0},{1,17},{17,1},{2,18},{18,2},{3,19},{19,3},{4,20},{20... | collective-permute-start | bytes 24584 | tf_op jit(solution)/shard_map/ppermute | solution.py:410
  5.1 2.3 constant_dynamic-slice_fusion
  7.5 0.2 copy.24
  7.7 1.6 copy.23
  9.3 1.1 fusion.1.freq_ref
  10.4 6.1 %collective-permute-start = (bf16[512,1152]{1,0:T(8,128)(2,1)}, bf16[512,1152]{1,0:T(8,128)(2,1)}, u32[]{:S(2)}, u32[]{:S(2)}) collective-permute-start(bf16[512,1152]{1,0:T(8,128)(2,1)} %fusion.1.freq_ref), channel_id=1, source_target_pairs={{0,8},{1,9},{2,10},{3,11},{4,12},{5,13},{6,14},{7,15},{24,16},{25,... | collective-permute-start | bytes 3538952 | tf_op jit(solution)/shard_map/ppermute | solution.py:443
  17.2 0.5 compare_select_fusion.1.pos_ref
  17.7 1.5 constant_dynamic-update-slice_fusion.2
  19.2 0.6 broadcast_xor_fusion.order_ref
  19.8 0.6 pad_add_fusion.place_ref
  20.4 1.4 copy.26.counter_ref
  21.8 1.4 copy.25.treated_ref
  23.2 9.1 %collective-permute-done.1 = bf16[512,1024]{1,0:T(8,128)(2,1)} collective-permute-done((bf16[512,1024]{1,0:T(8,128)(2,1)}, bf16[512,1024]{1,0:T(8,128)(2,1)}, u32[]{:S(2)}, u32[]{:S(2)}) %collective-permute-start.1) | collective-permute-done | bytes 1048608 | tf_op jit(solution)/shard_map/ppermute | solution.py:409
  32.3 2.3 constant_dynamic-update-slice_fusion.1
  34.6 5.9 %collective-permute-done = bf16[512,1152]{1,0:T(8,128)(2,1)} collective-permute-done((bf16[512,1152]{1,0:T(8,128)(2,1)}, bf16[512,1152]{1,0:T(8,128)(2,1)}, u32[]{:S(2)}, u32[]{:S(2)}) %collective-permute-start) | collective-permute-done | bytes 1179680 | tf_op jit(solution)/shard_map/ppermute | solution.py:443
  40.4 0.4 broadcast_select_fusion
  40.9 64.7 %shard_map.103.freq_ref = bf16[512,1152]{1,0:T(8,128)(2,1)S(1)} custom-call(bf16[512,1152]{1,0:T(8,128)(2,1)S(1)} %get-tuple-element.39.x_ref), custom_call_target="tpu_custom_call" | custom-call | flops 44999999488 | bytes 2000000 | tf_op jit(solution)/shard_map/pallas_call | solution.py:385
  105.6 1.0 copy-done
  106.6 1.0 constant_dynamic-update-slice_fusion.emb_ref.refs_8_
  107.7 12.1 %shard_map.104 = (bf16[2048,512]{1,0:T(8,128)(2,1)}, f32[1,512]{1,0:T(1,128)}) custom-call(s32[4]{0:T(128)} %compare_select_fusion.1.pos_ref, bf16[2048,1024]{1,0:T(8,128)(2,1)} %constant_dynamic-update-slice_fusion.emb_ref.refs_8_, bf16[512,1152]{1,0:T(8,128)(2,1)} %fusion.1.freq_ref, f32[2048,1]{1,0:T(8,128)} %copy.25.treated_ref, f32[2048,1]{1,0:T(8,128)} %copy.26.counter_ref), custom_call_target="tpu_custom_call" | custom-call | flops 2147483648 | bytes 4194304 | tf_op jit(solution)/shard_map/pallas_call | solution.py:67
  119.8 0.4 collective-permute-start.7
  120.1 2.6 collective-permute-start.6
  122.8 1.1 collective-permute-start.5
  123.9 12.0 %shard_map.105 = (bf16[2048,512]{1,0:T(8,128)(2,1)}, f32[1,512]{1,0:T(1,128)}) custom-call(s32[4]{0:T(128)} %compare_select_fusion.1.pos_ref, bf16[2048,1024]{1,0:T(8,128)(2,1)} %constant_dynamic-update-slice_fusion.emb_ref.refs_8_, bf16[512,1152]{1,0:T(8,128)(2,1)} %copy-done, f32[2048,1]{1,0:T(8,128)} %copy.25.treated_ref, f32[2048,1]{1,0:T(8,128)} %copy.26.counter_ref), custom_call_target="tpu_custom_call" | custom-call | flops 2147483648 | bytes 4194304 | tf_op jit(solution)/shard_map/pallas_call | solution.py:67
  135.9 27.5 %shard_map.106.x_in_ref = f32[512,1664]{1,0:T(8,128)} custom-call(s32[1]{0:T(128)} %bitcast.9.shift_ref, bf16[2048,512]{1,0:T(8,128)(2,1)} %get-tuple-element.24.feat_panel_ref.refs_11_, bf16[2048,512]{1,0:T(8,128)(2,1)} %get-tuple-element.25.feat_ref.refs_10_, f32[1,512]{1,0:T(1,128)} %get-tuple-element.26.moment_panel_ref), custom_call_target="tpu_custom_call" | custom-call | flops 20000000000 | bytes 8000000 | tf_op jit(solution)/shard_map/pallas_call | solution.py:196
  163.4 10.9 %collective-permute-done.5.refs_2_ = bf16[512,1152]{1,0:T(8,128)(2,1)S(1)} collective-permute-done((bf16[512,1152]{1,0:T(8,128)(2,1)S(1)}, bf16[512,1152]{1,0:T(8,128)(2,1)S(1)}, u32[]{:S(2)}, u32[]{:S(2)}) %collective-permute-start.5) | collective-permute-done | bytes 1179680 | tf_op jit(solution)/shard_map/ppermute | solution.py:402
  174.4 0.5 collective-permute-start.9
  175.0 22.5 %shard_map.107 = (bf16[512,512]{1,0:T(8,128)(2,1)}, bf16[512,512]{1,0:T(8,128)(2,1)}, bf16[512,512]{1,0:T(8,128)(2,1)}, bf16[512,512]{1,0:T(8,128)(2,1)}, f32[1,512]{1,0:T(1,128)}) custom-call(f32[512,1664]{1,0:T(8,128)} %shard_map.106.x_in_ref, f32[1,512]{1,0:T(1,128)} %get-tuple-element.31.moment_ref), custom_call_target="tpu_custom_call" | custom-call | flops 20000000000 | bytes 8000000 | tf_op jit(solution)/shard_map/pallas_call | solution.py:211
  197.5 1.0 copy-done.6
  198.5 67.7 %shard_map.108 = (f32[4096,512]{1,0:T(8,128)}, f32[4096,512]{1,0:T(8,128)}) custom-call(s32[8]{0:T(128)} %broadcast_xor_fusion.order_ref, s32[3]{0:T(128)} %pad_add_fusion.place_ref, s32[4]{0:T(128)} %compare_select_fusion.1.pos_ref, bf16[512,1152]{1,0:T(8,128)(2,1)} %copy-done.2, bf16[512,1152]{1,0:T(8,128)(2,1)} %copy-done.9, bf16[512,1152]{1,0:T(8,128)(2,1)} %copy-done.8, ...), custom_call_target="tpu_custom_call" | custom-call | flops 47244640256 | bytes 30000000 | tf_op jit(solution)/shard_map/pallas_call | solution.py:308
  (44 shorter events, 0.4 us)
Async XLA Ops:
  0.6 6.8 %copy-start.4 = (f32[512]{0:T(512)S(1)}, f32[512]{0:T(512)}, u32[]{:S(2)}) copy-start(f32[512]{0:T(512)} %param.11) | copy-start | bytes 6148
  0.6 6.7 %copy-start.5 = (f32[512]{0:T(512)S(1)}, f32[512]{0:T(512)}, u32[]{:S(2)}) copy-start(f32[512]{0:T(512)} %param.10) | copy-start | bytes 6148
  2.1 18.3 %collective-permute-start.3 = (f32[2,1024]{1,0:T(2,128)S(1)}, f32[2,1024]{1,0:T(2,128)S(1)}, u32[]{:S(2)}, u32[]{:S(2)}) collective-permute-start(f32[2,1024]{1,0:T(2,128)S(1)} %pad_maximum_fusion.1), channel_id=1, source_target_pairs={{0,16},{16,0},{1,17},{17,1},{2,18},{18,2},{3,19},{19,3},{4,20},{20... | collective-permute-start | bytes 24584 | tf_op jit(solution)/shard_map/ppermute | solution.py:410
  7.3 24.9 %collective-permute-start.1 = (bf16[512,1024]{1,0:T(8,128)(2,1)}, bf16[512,1024]{1,0:T(8,128)(2,1)}, u32[]{:S(2)}, u32[]{:S(2)}) collective-permute-start(bf16[512,1024]{1,0:T(8,128)(2,1)} %constant_dynamic-slice_fusion), channel_id=1, source_target_pairs={{0,16},{16,0},{1,17},{17,1},{2,18},{18,2},{3,19},{19,3},{4,20},{20... | collective-permute-start | bytes 3145736 | tf_op jit(solution)/shard_map/ppermute | solution.py:409
  7.7 10.0 %copy-start.1 = (bf16[1024,1024]{1,0:T(8,128)(2,1)S(1)}, bf16[1024,1024]{1,0:T(8,128)(2,1)}, u32[]{:S(2)}) copy-start(bf16[1024,1024]{1,0:T(8,128)(2,1)} %param.8) | copy-start | bytes 6291460
  10.4 30.0 %collective-permute-start = (bf16[512,1152]{1,0:T(8,128)(2,1)}, bf16[512,1152]{1,0:T(8,128)(2,1)}, u32[]{:S(2)}, u32[]{:S(2)}) collective-permute-start(bf16[512,1152]{1,0:T(8,128)(2,1)} %fusion.1.freq_ref), channel_id=1, source_target_pairs={{0,8},{1,9},{2,10},{3,11},{4,12},{5,13},{6,14},{7,15},{24,16},{25,... | collective-permute-start | bytes 3538952 | tf_op jit(solution)/shard_map/ppermute | solution.py:443
  17.7 1.5 copy-start.10
  20.4 14.1 %copy-start.3 = (f32[1,2048]{1,0:T(1,128)}, f32[1,2048]{1,0:T(1,128)S(1)}, u32[]{:S(2)}) copy-start(f32[1,2048]{1,0:T(1,128)S(1)} %get-tuple-element.42.refs_9_) | copy-start | bytes 24580
  32.3 74.3 %collective-permute-start.2 = (bf16[512,1024]{1,0:T(8,128)(2,1)}, bf16[512,1024]{1,0:T(8,128)(2,1)S(1)}, u32[]{:S(2)}, u32[]{:S(2)}) collective-permute-start(bf16[512,1024]{1,0:T(8,128)(2,1)} %collective-permute-done.1), channel_id=1, source_target_pairs={{0,1},{1,0},{2,3},{3,2},{4,5},{5,4},{6,7},{7,6},{8,9},{9,8},{10,11... | collective-permute-start | bytes 3145736 | tf_op jit(solution)/shard_map/ppermute | solution.py:402
  40.9 83.1 %copy-start.2 = (bf16[512,1152]{1,0:T(8,128)(2,1)}, bf16[512,1152]{1,0:T(8,128)(2,1)S(1)}, u32[]{:S(2)}) copy-start(bf16[512,1152]{1,0:T(8,128)(2,1)S(1)} %get-tuple-element.22.refs_0_) | copy-start | bytes 3538948
  105.6 1.0 copy-start
  119.8 77.7 %collective-permute-start.7 = (bf16[512,1152]{1,0:T(8,128)(2,1)S(1)}, bf16[512,1152]{1,0:T(8,128)(2,1)S(1)}, u32[]{:S(2)}, u32[]{:S(2)}) collective-permute-start(bf16[512,1152]{1,0:T(8,128)(2,1)S(1)} %get-tuple-element.22.refs_0_), channel_id=1, source_target_pairs={{0,1},{1,0},{2,3},{3,2},{4,5},{5,4},{6,7},{7,6},{8,9},{9,8},{10,11... | collective-permute-start | bytes 3538952 | tf_op jit(solution)/shard_map/ppermute | solution.py:402
  120.1 43.3 %collective-permute-start.6 = (bf16[512,1152]{1,0:T(8,128)(2,1)S(1)}, bf16[512,1152]{1,0:T(8,128)(2,1)S(1)}, u32[]{:S(2)}, u32[]{:S(2)}) collective-permute-start(bf16[512,1152]{1,0:T(8,128)(2,1)S(1)} %get-tuple-element.22.refs_0_), channel_id=1, source_target_pairs={{0,6},{1,7},{2,4},{3,5},{4,2},{5,3},{6,0},{7,1},{8,14},{9,15},{10,... | collective-permute-start | bytes 3538952 | tf_op jit(solution)/shard_map/ppermute | solution.py:402
  122.8 51.6 %collective-permute-start.5 = (bf16[512,1152]{1,0:T(8,128)(2,1)S(1)}, bf16[512,1152]{1,0:T(8,128)(2,1)S(1)}, u32[]{:S(2)}, u32[]{:S(2)}) collective-permute-start(bf16[512,1152]{1,0:T(8,128)(2,1)S(1)} %get-tuple-element.22.refs_0_), channel_id=1, source_target_pairs={{0,2},{1,3},{2,0},{3,1},{4,6},{5,7},{6,4},{7,5},{8,10},{9,11},{10,... | collective-permute-start | bytes 3538952 | tf_op jit(solution)/shard_map/ppermute | solution.py:402
  123.9 50.4 %collective-permute-start.4 = (bf16[512,1152]{1,0:T(8,128)(2,1)S(1)}, bf16[512,1152]{1,0:T(8,128)(2,1)S(1)}, u32[]{:S(2)}, u32[]{:S(2)}) collective-permute-start(bf16[512,1152]{1,0:T(8,128)(2,1)S(1)} %get-tuple-element.22.refs_0_), channel_id=1, source_target_pairs={{0,4},{1,5},{2,6},{3,7},{4,0},{5,1},{6,2},{7,3},{8,12},{9,13},{10,... | collective-permute-start | bytes 3538952 | tf_op jit(solution)/shard_map/ppermute | solution.py:402
  163.4 34.0 %copy-start.7 = (bf16[512,1152]{1,0:T(8,128)(2,1)}, bf16[512,1152]{1,0:T(8,128)(2,1)S(1)}, u32[]{:S(2)}) copy-start(bf16[512,1152]{1,0:T(8,128)(2,1)S(1)} %collective-permute-done.6.refs_3_) | copy-start | bytes 3538948
  174.4 23.1 %copy-start.8 = (bf16[512,1152]{1,0:T(8,128)(2,1)}, bf16[512,1152]{1,0:T(8,128)(2,1)S(1)}, u32[]{:S(2)}) copy-start(bf16[512,1152]{1,0:T(8,128)(2,1)S(1)} %collective-permute-done.5.refs_2_) | copy-start | bytes 3538948
  174.4 23.1 %copy-start.9 = (bf16[512,1152]{1,0:T(8,128)(2,1)}, bf16[512,1152]{1,0:T(8,128)(2,1)S(1)}, u32[]{:S(2)}) copy-start(bf16[512,1152]{1,0:T(8,128)(2,1)S(1)} %collective-permute-done.4.refs_1_) | copy-start | bytes 3538948
  174.4 23.1 %collective-permute-start.8 = (bf16[512,1152]{1,0:T(8,128)(2,1)S(1)}, bf16[512,1152]{1,0:T(8,128)(2,1)}, u32[]{:S(2)}, u32[]{:S(2)}) collective-permute-start(bf16[512,1152]{1,0:T(8,128)(2,1)S(1)} %collective-permute-done.4.refs_1_), channel_id=1, source_target_pairs={{0,1},{1,0},{2,3},{3,2},{4,5},{5,4},{6,7},{7,6},{8,9},{9,8},{10,11... | collective-permute-start | bytes 3538952 | tf_op jit(solution)/shard_map/ppermute | solution.py:402
  174.4 23.1 %collective-permute-start.9 = (bf16[512,1152]{1,0:T(8,128)(2,1)S(1)}, bf16[512,1152]{1,0:T(8,128)(2,1)}, u32[]{:S(2)}, u32[]{:S(2)}) collective-permute-start(bf16[512,1152]{1,0:T(8,128)(2,1)S(1)} %collective-permute-done.5.refs_2_), channel_id=1, source_target_pairs={{0,1},{1,0},{2,3},{3,2},{4,5},{5,4},{6,7},{7,6},{8,9},{9,8},{10,11... | collective-permute-start | bytes 3538952 | tf_op jit(solution)/shard_map/ppermute | solution.py:402
  174.9 22.6 %collective-permute-start.10 = (bf16[512,1152]{1,0:T(8,128)(2,1)S(1)}, bf16[512,1152]{1,0:T(8,128)(2,1)}, u32[]{:S(2)}, u32[]{:S(2)}) collective-permute-start(bf16[512,1152]{1,0:T(8,128)(2,1)S(1)} %collective-permute-done.6.refs_3_), channel_id=1, source_target_pairs={{0,1},{1,0},{2,3},{3,2},{4,5},{5,4},{6,7},{7,6},{8,9},{9,8},{10,11... | collective-permute-start | bytes 3538952 | tf_op jit(solution)/shard_map/ppermute | solution.py:402
  197.5 1.0 copy-start.6

commit v4 on v3

--- a/solution.py
+++ b/solution.py
@@ -327,7 +327,9 @@
     )(order, place, pos, *freqs, emb, treated, feat, feat_panel, *solved)
 
 
-def spread_kernel(axis_size, x_ref, out_ref, sums, arrived, send_sems, recv_sems):
+def entry_kernel(
+    axis_size, x_ref, freq_ref, emb_ref, out_ref, mine_ref, all_ref, sums, arrived, send_sems, recv_sems, local_sems
+):
     samp, feat = lax.axis_index("samp"), lax.axis_index("feat")
     rows = x_ref.shape[0]
     bits = []
@@ -339,19 +341,50 @@
     barrier = pltpu.get_barrier_semaphore()
     for mate in mates:
         pl.semaphore_signal(barrier, inc=1, device_id=(samp, mate), device_id_type=pl.DeviceIdType.MESH)
-    pl.semaphore_wait(barrier, len(bits))
-
-    def send(source, target, mate, index):
-        copy = pltpu.make_async_remote_copy(
+    pl.semaphore_signal(barrier, inc=1, device_id=(1 - samp, feat), device_id_type=pl.DeviceIdType.MESH)
+    pl.semaphore_wait(barrier, len(bits) + 1)
+
+    def remote(source, target, device, index):
+        return pltpu.make_async_remote_copy(
             src_ref=source,
             dst_ref=target,
             send_sem=send_sems.at[index],
             recv_sem=recv_sems.at[index],
-            device_id=(samp, mate),
+            device_id=device,
             device_id_type=pl.DeviceIdType.MESH,
         )
+
+    def send(source, target, mate, index):
+        copy = remote(source, target, (samp, mate), index)
         copy.start()
         copy.wait()
+
+    steps = 2 * len(bits)
+    count = emb_ref.shape[0]
+    part_rows = count // 2
+    core = feat % 2
+    mine_at = pl.multiple_of(samp * count + core * part_rows, 16)
+    other_at = pl.multiple_of((1 - samp) * count + core * part_rows, 16)
+    across = remote(
+        emb_ref.at[pl.ds(pl.multiple_of(core * part_rows, 16), part_rows)],
+        all_ref.at[pl.ds(mine_at, part_rows)],
+        (1 - samp, feat),
+        steps,
+    )
+    across.start()
+    keeps = feat // (axis_size // 2) == samp
+    crossing = remote(freq_ref, mine_ref, (samp, mates[-1]), steps + 1)
+    keep = pltpu.make_async_copy(freq_ref, mine_ref, local_sems.at[0])
+    stay = pltpu.make_async_copy(
+        emb_ref, all_ref.at[pl.ds(pl.multiple_of(samp * count, 16), count)], local_sems.at[1]
+    )
+
+    @pl.when(keeps)
+    def _():
+        crossing.start()
+        keep.start()
+
+    stay.start()
 
     first = 0
     firsts = []
@@ -377,43 +410,50 @@
         first, size = firsts[index]
         part = out_ref.at[pl.ds(first, size)]
         send(part, part, mates[index], len(bits) + index)
-
-
-def spread(x):
+    across.wait()
+    fetched = all_ref.at[pl.ds(other_at, part_rows)]
+    forward = remote(fetched, fetched, (samp, mates[0]), steps + 2)
+    forward.start()
+    forward.wait()
+    stay.wait()
+
+    @pl.when(keeps)
+    def _():
+        crossing.wait_send()
+        keep.wait()
+
+    @pl.when(jnp.logical_not(keeps))
+    def _():
+        crossing.wait_recv()
+
+
+def enter(x, freq_t, emb):
     axis_size = lax.axis_size("feat")
-    steps = 2 * (axis_size.bit_length() - 1)
+    steps = 2 * (axis_size.bit_length() - 1) + 3
+    vmem, anywhere = pl.BlockSpec(memory_space=pltpu.VMEM), pl.BlockSpec(memory_space=pl.ANY)
     return pl.pallas_call(
-        functools.partial(spread_kernel, axis_size),
-        in_specs=[pl.BlockSpec(memory_space=pltpu.VMEM)],
-        out_specs=pl.BlockSpec(memory_space=pltpu.VMEM),
-        out_shape=jax.ShapeDtypeStruct(x.shape, x.dtype),
+        functools.partial(entry_kernel, axis_size),
+        in_specs=[vmem, anywhere, anywhere],
+        out_specs=[vmem, anywhere, anywhere],
+        out_shape=[
+            jax.ShapeDtypeStruct(x.shape, x.dtype),
+            jax.ShapeDtypeStruct(freq_t.shape, freq_t.dtype),
+            jax.ShapeDtypeStruct((2 * emb.shape[0], emb.shape[1]), emb.dtype),
+        ],
         scratch_shapes=[
             pltpu.VMEM(x.shape, x.dtype),
             pltpu.VMEM(x.shape, x.dtype),
             pltpu.SemaphoreType.DMA((steps,)),
             pltpu.SemaphoreType.DMA((steps,)),
+            pltpu.SemaphoreType.DMA((2,)),
         ],
         cost_estimate=pl.CostEstimate(flops=45 * 10**9, bytes_accessed=2 * 10**6, transcendentals=0),
         compiler_params=pltpu.CompilerParams(collective_id=0, has_side_effects=True, vmem_limit_bytes=16 * 1024 * 1024),
-    )(x)
+    )(x, freq_t, emb)
 
 
 def swap(value, bits):
     return lax.ppermute(value, "feat", [(f, f ^ bits) for f in range(lax.axis_size("feat"))])
-
-
-def gather_samples_staged(embeddings, marks, samp_index, feat_index):
-    part = embeddings.shape[0] // 2
-    core = feat_index % 2
-    mine = lax.dynamic_slice_in_dim(embeddings, core * part, part, 0)
-    got = lax.ppermute(mine, "samp", [(0, 1), (1, 0)])
-    other_marks = lax.ppermute(marks, "samp", [(0, 1), (1, 0)])
-    emb = jnp.concatenate([embeddings, got, swap(got, 1)], axis=0)
-    piece = jnp.arange(4, dtype=jnp.int32)
-    pos = jnp.where(piece // 2 == samp_index, piece % 2, jnp.where(piece % 2 == core, 2, 3))
-    first = samp_index == 0
-    marks = jnp.concatenate([jnp.where(first, marks, other_marks), jnp.where(first, other_marks, marks)], axis=1)
-    return emb, marks, pos.astype(jnp.int32)
 
 
 def per_device(embeddings, frequencies, phases, treat_freq, treatment, flips, panel):
@@ -438,29 +478,24 @@
     counter = treated + flipped - 2.0 * treated * flipped
     marks = jnp.stack([treated, counter])
     if staged:
-        emb, marks, pos = gather_samples_staged(embeddings, marks, samp_index, feat_index)
-        mates = [(s * 16 + f, s * 16 + (f ^ half)) for s in range(2) for f in range(s * half, (s + 1) * half)]
-        crossed = lax.ppermute(freq_t, ("samp", "feat"), mates)
-        mine = jnp.where(feat_index // half == samp_index, freq_t, crossed)
+        masked = jnp.where(feat_index == first_dev, freq_t, jnp.zeros_like(freq_t))
+        other_marks = lax.ppermute(marks, "samp", [(0, 1), (1, 0)])
+        first = samp_index == 0
+        marks = jnp.concatenate([jnp.where(first, marks, other_marks), jnp.where(first, other_marks, marks)], axis=1)
+        panel_freq, mine, emb = enter(masked, freq_t, embeddings)
+        near = [swap(mine, 4), swap(mine, 2), swap(mine, 6)]
     else:
         emb = lax.all_gather(embeddings, "samp", axis=0, tiled=True)
         marks = lax.all_gather(marks, "samp", axis=1, tiled=True)
-        pos = jnp.arange(emb.shape[0] // 512, dtype=jnp.int32)
-
-    if staged:
-        panel_freq = spread(jnp.where(feat_index == first_dev, freq_t, jnp.zeros_like(freq_t)))
-    else:
         panel_freq = []
         for member in range(PANEL // col_width):
             own = feat_index == first_dev + member
             panel_freq.append(lax.psum(jnp.where(own, freq_t, jnp.zeros_like(freq_t)), "feat"))
         panel_freq = jnp.concatenate(panel_freq, axis=0)
+    pos = jnp.arange(emb.shape[0] // 512, dtype=jnp.int32)
 
     treated_col, counter_col = marks[0][:, None], marks[1][:, None]
     feat, moment = make_features(pos, emb, freq_t, treated_col, counter_col)
-    if staged:
-        mine, panel_freq, feat = lax.optimization_barrier((mine, panel_freq, feat))
-        near = [swap(mine, 4), swap(mine, 2), swap(mine, 6)]
     feat_panel, moment_panel = make_features(pos, emb, panel_freq, treated_col, counter_col)
     own_col = feat_index * col_width
     shift = (own_col - first_col).reshape(1).astype(jnp.int32)

time: 267 us -> 247 us (0.925)
  waiting for transfers between devices: 25.9 us -> 2.44 us
  Pallas kernels: 206 us -> 223 us
  starting transfers between devices: 13.9 us -> 4.36 us
    pallas_call x1, Pallas kernels: 64.7 us -> 81.8 us  [enter(): pl.pallas_call(functools.partial(entry_kernel, axis_size), in_specs=[vmem...]
    ppermute x3 -> x1, waiting for transfers between devices: 15 us -> 2.42 us  [per_device(): other_marks = lax.ppermute(marks, 'samp', [(0, 1), (1, 0)])]
    ppermute x8 -> x7, waiting for transfers between devices: 10.9 us -> 0.02 us  [swap(): lax.ppermute(value, 'feat', [(f, f ^ bits) for f in range(lax.axis_size('...]
    ppermute x3 -> x1, starting transfers between devices: 9.09 us -> 0.07 us  [per_device(): other_marks = lax.ppermute(marks, 'samp', [(0, 1), (1, 0)])]
    unnamed x25 -> x27, local copies, waits for them, and re-layouts: 7.47 us -> 7.62 us
  transfers between devices with their start and end apart: 11 -> 8, of which waited for: 3 -> 1; matrix products, arithmetic and copies ran while one was open for 5% -> 2% of each run, Pallas kernels for 48% -> 30%
where the time goes in v4:
time: 247 us; the launch traced here: 246 us
  Pallas kernels  223 us (90%)
  local copies, waits for them, and re-layouts  12.2 us (5%)
  starting transfers between devices  4.36 us (2%)
    pallas_call x1, Pallas kernels, enter(): pl.pallas_call(functools.partial(entry_kernel, axis_size), in_specs=[vmem...  81.8 us
    pallas_call x1, Pallas kernels, main(): pl.pallas_call(functools.partial(main_kernel, count, blocks), grid_spec=p...  67.7 us
    pallas_call x1, Pallas kernels, eliminate_front(): pl.pallas_call(functools.partial(front_kernel, count), in_specs=[pl.Block...  27.7 us
    pallas_call x2, Pallas kernels, make_features(): pl.pallas_call(feature_kernel, grid_spec=pltpu.PrefetchScalarGridSpec(num...  23.9 us
    pallas_call x1, Pallas kernels, eliminate_back(): pl.pallas_call(functools.partial(back_kernel, count), in_specs=[vmem] * 2...  22.1 us
    unnamed x27, local copies, waits for them, and re-layouts  7.62 us
  transfers between devices with their start and end apart: 8, of which 1 were waited for; matrix products, arithmetic and copies ran while one was open for 2% of the time, Pallas kernels for 30%

profile of v4, /device:TPU:0, one launch (start us, length us, event | category | flops | bytes accessed | tf_op | source)
XLA Modules:
  0.0 246.1 jit_solution(4638269450250128495)
XLA Ops:
  1.3 0.7 fusion.5
  2.1 0.2 copy.24
  2.3 1.5 copy.23
  3.8 0.3 fusion.1
  4.2 1.7 copy-done.1
  5.8 81.8 %shard_map.103 = (bf16[512,1152]{1,0:T(8,128)(2,1)S(1)}, bf16[512,1152]{1,0:T(8,128)(2,1)S(1)}, bf16[2048,1024]{1,0:T(8,128)(2,1)S(1)}) custom-call(bf16[512,1152]{1,0:T(8,128)(2,1)S(1)} %get-tuple-element.40.x_ref, bf16[512,1152]{1,0:T(8,128)(2,1)S(1)} %get-tuple-element.39.freq_ref, bf16[1024,1024]{1,0:T(8,128)(2,1)S(1)} %copy-done.1), custom_call_target="tpu_custom_call" | custom-call | flops 44999999488 | bytes 2000000 | tf_op jit(solution)/shard_map/pallas_call | solution.py:434
  87.6 1.9 copy-done.3
  89.6 1.0 copy-done.4
  90.6 0.1 collective-permute-start.4
  90.7 0.9 collective-permute-start.2
  91.7 2.6 %collective-permute-start.1 = (bf16[512,1152]{1,0:T(8,128)(2,1)S(1)}, bf16[512,1152]{1,0:T(8,128)(2,1)}, u32[]{:S(2)}, u32[]{:S(2)}) collective-permute-start(bf16[512,1152]{1,0:T(8,128)(2,1)S(1)} %get-tuple-element.21.refs_0_), channel_id=1, source_target_pairs={{0,4},{1,5},{2,6},{3,7},{4,0},{5,1},{6,2},{7,3},{8,12},{9,13},{10,... | collective-permute-start | bytes 3538952 | tf_op jit(solution)/shard_map/ppermute | solution.py:456
  94.3 0.1 collective-permute-start
  94.4 0.5 broadcast_xor_fusion.order_ref
  94.9 0.7 pad_add_fusion.place_ref
  95.5 2.4 collective-permute-done
  98.0 1.4 copy.26.counter_ref
  99.4 1.3 copy.25.treated_ref
  100.7 0.5 iota.9.pos_ref
  101.2 12.0 %shard_map.105 = (bf16[2048,512]{1,0:T(8,128)(2,1)}, f32[1,512]{1,0:T(1,128)}) custom-call(s32[4]{0:T(128)} %iota.9.pos_ref, bf16[2048,1024]{1,0:T(8,128)(2,1)} %copy-done.3, bf16[512,1152]{1,0:T(8,128)(2,1)} %copy-done, f32[2048,1]{1,0:T(8,128)} %copy.25.treated_ref, f32[2048,1]{1,0:T(8,128)} %copy.26.counter_ref), custom_call_target="tpu_custom_call" | custom-call | flops 2147483648 | bytes 4194304 | tf_op jit(solution)/shard_map/pallas_call | solution.py:67
  113.2 0.5 iota.8.pos_ref
  113.7 12.0 %shard_map.104 = (bf16[2048,512]{1,0:T(8,128)(2,1)}, f32[1,512]{1,0:T(1,128)}) custom-call(s32[4]{0:T(128)} %iota.8.pos_ref, bf16[2048,1024]{1,0:T(8,128)(2,1)} %copy-done.3, bf16[512,1152]{1,0:T(8,128)(2,1)} %copy-done.4, f32[2048,1]{1,0:T(8,128)} %copy.25.treated_ref, f32[2048,1]{1,0:T(8,128)} %copy.26.counter_ref), custom_call_target="tpu_custom_call" | custom-call | flops 2147483648 | bytes 4194304 | tf_op jit(solution)/shard_map/pallas_call | solution.py:67
  125.7 27.7 %shard_map.106.x_in_ref = f32[512,1664]{1,0:T(8,128)} custom-call(s32[1]{0:T(128)} %bitcast.5.shift_ref, bf16[2048,512]{1,0:T(8,128)(2,1)} %get-tuple-element.24.feat_panel_ref.refs_11_, bf16[2048,512]{1,0:T(8,128)(2,1)} %get-tuple-element.25.feat_ref.refs_10_, f32[1,512]{1,0:T(1,128)} %get-tuple-element.26.moment_panel_ref), custom_call_target="tpu_custom_call" | custom-call | flops 20000000000 | bytes 8000000 | tf_op jit(solution)/shard_map/pallas_call | solution.py:196
  153.4 0.1 collective-permute-start.5
  153.5 0.5 collective-permute-start.6
  154.0 0.1 collective-permute-start.7
  154.1 22.1 %shard_map.107 = (bf16[512,512]{1,0:T(8,128)(2,1)}, bf16[512,512]{1,0:T(8,128)(2,1)}, bf16[512,512]{1,0:T(8,128)(2,1)}, bf16[512,512]{1,0:T(8,128)(2,1)}, f32[1,512]{1,0:T(1,128)}) custom-call(f32[512,1664]{1,0:T(8,128)} %shard_map.106.x_in_ref, f32[1,512]{1,0:T(1,128)} %get-tuple-element.31.moment_ref), custom_call_target="tpu_custom_call" | custom-call | flops 20000000000 | bytes 8000000 | tf_op jit(solution)/shard_map/pallas_call | solution.py:211
  176.2 0.6 iota.7.pos_ref
  176.8 0.4 copy-done.8
  177.2 0.4 copy-done.9
  177.5 0.4 copy-done.10
  177.9 0.4 copy-done.11
  178.3 67.7 %shard_map.108 = (f32[4096,512]{1,0:T(8,128)}, f32[4096,512]{1,0:T(8,128)}) custom-call(s32[8]{0:T(128)} %broadcast_xor_fusion.order_ref, s32[3]{0:T(128)} %pad_add_fusion.place_ref, s32[4]{0:T(128)} %iota.7.pos_ref, bf16[512,1152]{1,0:T(8,128)(2,1)} %copy-done.2, bf16[512,1152]{1,0:T(8,128)(2,1)} %collective-permute-done.1.refs_1_, ...), custom_call_target="tpu_custom_call" | custom-call | flops 47244640256 | bytes 30000000 | tf_op jit(solution)/shard_map/pallas_call | solution.py:308
  (39 shorter events, 0.2 us)
Async XLA Ops:
  3.8 2.0 copy-start.1
  4.1 83.5 %copy-start = (bf16[512,1152]{1,0:T(8,128)(2,1)}, bf16[512,1152]{1,0:T(8,128)(2,1)S(1)}, u32[]{:S(2)}) copy-start(bf16[512,1152]{1,0:T(8,128)(2,1)S(1)} %get-tuple-element.39.freq_ref) | copy-start | bytes 3538948
  5.8 88.4 %copy-start.6 = (s32[1024]{0:T(1024)S(1)}, s32[1024]{0:T(1024)}, u32[]{:S(2)}) copy-start(s32[1024]{0:T(1024)} %param.12) | copy-start | bytes 12292
  5.8 88.4 %copy-start.7 = (s32[1024]{0:T(1024)S(1)}, s32[1024]{0:T(1024)}, u32[]{:S(2)}) copy-start(s32[1024]{0:T(1024)} %param.13) | copy-start | bytes 12292
  5.8 88.5 %copy-start.12 = (s32[8]{0:T(128)S(1)}, s32[8]{0:T(128)}, u32[]{:S(2)}) copy-start(s32[8]{0:T(128)} %constant.52.clone) | copy-start | bytes 100
  87.6 2.0 copy-start.3
  89.6 1.0 copy-start.4
  90.6 22.6 %copy-start.2 = (bf16[512,1152]{1,0:T(8,128)(2,1)}, bf16[512,1152]{1,0:T(8,128)(2,1)S(1)}, u32[]{:S(2)}) copy-start(bf16[512,1152]{1,0:T(8,128)(2,1)S(1)} %get-tuple-element.21.refs_0_) | copy-start | bytes 3538948
  90.6 85.6 %collective-permute-start.4 = (bf16[512,1152]{1,0:T(8,128)(2,1)S(1)}, bf16[512,1152]{1,0:T(8,128)(2,1)S(1)}, u32[]{:S(2)}, u32[]{:S(2)}) collective-permute-start(bf16[512,1152]{1,0:T(8,128)(2,1)S(1)} %get-tuple-element.21.refs_0_), channel_id=1, source_target_pairs={{0,1},{1,0},{2,3},{3,2},{4,5},{5,4},{6,7},{7,6},{8,9},{9,8},{10,11... | collective-permute-start | bytes 3538952 | tf_op jit(solution)/shard_map/ppermute | solution.py:456
  90.7 62.7 %collective-permute-start.3 = (bf16[512,1152]{1,0:T(8,128)(2,1)S(1)}, bf16[512,1152]{1,0:T(8,128)(2,1)}, u32[]{:S(2)}, u32[]{:S(2)}) collective-permute-start(bf16[512,1152]{1,0:T(8,128)(2,1)S(1)} %get-tuple-element.21.refs_0_), channel_id=1, source_target_pairs={{0,6},{1,7},{2,4},{3,5},{4,2},{5,3},{6,0},{7,1},{8,14},{9,15},{10,... | collective-permute-start | bytes 3538952 | tf_op jit(solution)/shard_map/ppermute | solution.py:456
  90.7 62.7 %collective-permute-start.2 = (bf16[512,1152]{1,0:T(8,128)(2,1)S(1)}, bf16[512,1152]{1,0:T(8,128)(2,1)}, u32[]{:S(2)}, u32[]{:S(2)}) collective-permute-start(bf16[512,1152]{1,0:T(8,128)(2,1)S(1)} %get-tuple-element.21.refs_0_), channel_id=1, source_target_pairs={{0,2},{1,3},{2,0},{3,1},{4,6},{5,7},{6,4},{7,5},{8,10},{9,11},{10,... | collective-permute-start | bytes 3538952 | tf_op jit(solution)/shard_map/ppermute | solution.py:456
  91.7 61.7 %collective-permute-start.1 = (bf16[512,1152]{1,0:T(8,128)(2,1)S(1)}, bf16[512,1152]{1,0:T(8,128)(2,1)}, u32[]{:S(2)}, u32[]{:S(2)}) collective-permute-start(bf16[512,1152]{1,0:T(8,128)(2,1)S(1)} %get-tuple-element.21.refs_0_), channel_id=1, source_target_pairs={{0,4},{1,5},{2,6},{3,7},{4,0},{5,1},{6,2},{7,3},{8,12},{9,13},{10,... | collective-permute-start | bytes 3538952 | tf_op jit(solution)/shard_map/ppermute | solution.py:456
  94.3 3.7 %collective-permute-start = (f32[2,1024]{1,0:T(2,128)S(1)}, f32[2,1024]{1,0:T(2,128)S(1)}, u32[]{:S(2)}, u32[]{:S(2)}) collective-permute-start(f32[2,1024]{1,0:T(2,128)S(1)} %pad_maximum_fusion.1), channel_id=1, source_target_pairs={{0,16},{16,0},{1,17},{17,1},{2,18},{18,2},{3,19},{19,3},{4,20},{20... | collective-permute-start | bytes 24584 | tf_op jit(solution)/shard_map/ppermute | solution.py:482
  98.0 15.2 %copy-start.5 = (f32[1,2048]{1,0:T(1,128)}, f32[1,2048]{1,0:T(1,128)S(1)}, u32[]{:S(2)}) copy-start(f32[1,2048]{1,0:T(1,128)S(1)} %get-tuple-element.42.refs_9_) | copy-start | bytes 24580
  153.4 22.8 %collective-permute-start.5 = (bf16[512,1152]{1,0:T(8,128)(2,1)}, bf16[512,1152]{1,0:T(8,128)(2,1)S(1)}, u32[]{:S(2)}, u32[]{:S(2)}) collective-permute-start(bf16[512,1152]{1,0:T(8,128)(2,1)} %collective-permute-done.1.refs_1_), channel_id=1, source_target_pairs={{0,1},{1,0},{2,3},{3,2},{4,5},{5,4},{6,7},{7,6},{8,9},{9,8},{10,11... | collective-permute-start | bytes 3538952 | tf_op jit(solution)/shard_map/ppermute | solution.py:456
  153.5 22.7 %collective-permute-start.6 = (bf16[512,1152]{1,0:T(8,128)(2,1)}, bf16[512,1152]{1,0:T(8,128)(2,1)S(1)}, u32[]{:S(2)}, u32[]{:S(2)}) collective-permute-start(bf16[512,1152]{1,0:T(8,128)(2,1)} %collective-permute-done.2.refs_2_), channel_id=1, source_target_pairs={{0,1},{1,0},{2,3},{3,2},{4,5},{5,4},{6,7},{7,6},{8,9},{9,8},{10,11... | collective-permute-start | bytes 3538952 | tf_op jit(solution)/shard_map/ppermute | solution.py:456
  154.0 22.2 %collective-permute-start.7 = (bf16[512,1152]{1,0:T(8,128)(2,1)}, bf16[512,1152]{1,0:T(8,128)(2,1)S(1)}, u32[]{:S(2)}, u32[]{:S(2)}) collective-permute-start(bf16[512,1152]{1,0:T(8,128)(2,1)} %collective-permute-done.3.refs_3_), channel_id=1, source_target_pairs={{0,1},{1,0},{2,3},{3,2},{4,5},{5,4},{6,7},{7,6},{8,9},{9,8},{10,11... | collective-permute-start | bytes 3538952 | tf_op jit(solution)/shard_map/ppermute | solution.py:456
  176.1 1.0 copy-start.8
  176.2 1.4 copy-start.9
  176.2 1.7 copy-start.10
  176.2 2.1 copy-start.11

commit v5 on v4

--- a/solution.py
+++ b/solution.py
@@ -379,11 +379,6 @@
         emb_ref, all_ref.at[pl.ds(pl.multiple_of(samp * count, 16), count)], local_sems.at[1]
     )
 
-    @pl.when(keeps)
-    def _():
-        crossing.start()
-        keep.start()
-
     stay.start()
 
     first = 0
@@ -410,6 +405,13 @@
         first, size = firsts[index]
         part = out_ref.at[pl.ds(first, size)]
         send(part, part, mates[index], len(bits) + index)
+        if index == len(bits) - 1:
+
+            @pl.when(keeps)
+            def _():
+                crossing.start()
+                keep.start()
+
     across.wait()
     fetched = all_ref.at[pl.ds(other_at, part_rows)]
     forward = remote(fetched, fetched, (samp, mates[0]), steps + 2)

time: 247 us -> 244 us (0.988)
  Pallas kernels: 223 us -> 207 us
  starting transfers between devices: 4.36 us -> 19.2 us
    pallas_call x1, Pallas kernels: 81.8 us -> 66.1 us  [enter(): pl.pallas_call(functools.partial(entry_kernel, axis_size), in_specs=[vmem...]
    ppermute x7, starting transfers between devices: 4.29 us -> 15.1 us  [swap(): lax.ppermute(value, 'feat', [(f, f ^ bits) for f in range(lax.axis_size('...]
    ppermute x1, starting transfers between devices: 0.07 us -> 4.08 us  [per_device(): other_marks = lax.ppermute(marks, 'samp', [(0, 1), (1, 0)])]
where the time goes in v5:
time: 244 us; the launch traced here: 243 us
  Pallas kernels  207 us (85%)
  starting transfers between devices  19.2 us (8%)
  local copies, waits for them, and re-layouts  12.2 us (5%)
    pallas_call x1, Pallas kernels, main(): pl.pallas_call(functools.partial(main_kernel, count, blocks), grid_spec=p...  67.7 us
    pallas_call x1, Pallas kernels, enter(): pl.pallas_call(functools.partial(entry_kernel, axis_size), in_specs=[vmem...  66.1 us
    pallas_call x1, Pallas kernels, eliminate_front(): pl.pallas_call(functools.partial(front_kernel, count), in_specs=[pl.Block...  27.5 us
    pallas_call x2, Pallas kernels, make_features(): pl.pallas_call(feature_kernel, grid_spec=pltpu.PrefetchScalarGridSpec(num...  23.9 us
    pallas_call x1, Pallas kernels, eliminate_back(): pl.pallas_call(functools.partial(back_kernel, count), in_specs=[vmem] * 2...  22.3 us
    ppermute x7, starting transfers between devices, swap(): lax.ppermute(value, 'feat', [(f, f ^ bits) for f in range(lax.axis_size('...  15.1 us
    unnamed x27, local copies, waits for them, and re-layouts  7.62 us
  transfers between devices with their start and end apart: 8, of which 1 were waited for; matrix products, arithmetic and copies ran while one was open for 2% of the time, Pallas kernels for 30%

profile of v5, /device:TPU:0, one launch (start us, length us, event | category | flops | bytes accessed | tf_op | source)
XLA Modules:
  0.0 243.2 jit_solution(12369613269538445111)
XLA Ops:
  1.3 0.7 fusion.5
  2.1 0.2 copy.24
  2.3 1.5 copy.23
  3.8 0.3 fusion.1
  4.2 1.7 copy-done.1
  5.8 66.1 %shard_map.103 = (bf16[512,1152]{1,0:T(8,128)(2,1)S(1)}, bf16[512,1152]{1,0:T(8,128)(2,1)S(1)}, bf16[2048,1024]{1,0:T(8,128)(2,1)S(1)}) custom-call(bf16[512,1152]{1,0:T(8,128)(2,1)S(1)} %get-tuple-element.40.x_ref, bf16[512,1152]{1,0:T(8,128)(2,1)S(1)} %get-tuple-element.39.freq_ref, bf16[1024,1024]{1,0:T(8,128)(2,1)S(1)} %copy-done.1), custom_call_target="tpu_custom_call" | custom-call | flops 44999999488 | bytes 2000000 | tf_op jit(solution)/shard_map/pallas_call | solution.py:436
  71.9 1.9 copy-done.3
  73.9 1.0 copy-done.4
  74.9 0.1 collective-permute-start.4
  75.1 12.8 %collective-permute-start.3 = (bf16[512,1152]{1,0:T(8,128)(2,1)S(1)}, bf16[512,1152]{1,0:T(8,128)(2,1)}, u32[]{:S(2)}, u32[]{:S(2)}) collective-permute-start(bf16[512,1152]{1,0:T(8,128)(2,1)S(1)} %get-tuple-element.21.refs_0_), channel_id=1, source_target_pairs={{0,6},{1,7},{2,4},{3,5},{4,2},{5,3},{6,0},{7,1},{8,14},{9,15},{10,... | collective-permute-start | bytes 3538952 | tf_op jit(solution)/shard_map/ppermute | solution.py:458
  87.8 1.5 collective-permute-start.2
  89.4 4.1 %collective-permute-start = (f32[2,1024]{1,0:T(2,128)S(1)}, f32[2,1024]{1,0:T(2,128)S(1)}, u32[]{:S(2)}, u32[]{:S(2)}) collective-permute-start(f32[2,1024]{1,0:T(2,128)S(1)} %pad_maximum_fusion.1), channel_id=1, source_target_pairs={{0,16},{16,0},{1,17},{17,1},{2,18},{18,2},{3,19},{19,3},{4,20},{20... | collective-permute-start | bytes 24584 | tf_op jit(solution)/shard_map/ppermute | solution.py:484
  93.5 0.5 broadcast_xor_fusion.order_ref
  94.0 0.7 pad_add_fusion.place_ref
  94.7 0.4 collective-permute-done
  95.2 1.4 copy.26.counter_ref
  96.5 1.3 copy.25.treated_ref
  97.9 0.5 iota.9.pos_ref
  98.4 12.0 %shard_map.105 = (bf16[2048,512]{1,0:T(8,128)(2,1)}, f32[1,512]{1,0:T(1,128)}) custom-call(s32[4]{0:T(128)} %iota.9.pos_ref, bf16[2048,1024]{1,0:T(8,128)(2,1)} %copy-done.3, bf16[512,1152]{1,0:T(8,128)(2,1)} %copy-done, f32[2048,1]{1,0:T(8,128)} %copy.25.treated_ref, f32[2048,1]{1,0:T(8,128)} %copy.26.counter_ref), custom_call_target="tpu_custom_call" | custom-call | flops 2147483648 | bytes 4194304 | tf_op jit(solution)/shard_map/pallas_call | solution.py:67
  110.4 0.5 iota.8.pos_ref
  110.9 12.0 %shard_map.104 = (bf16[2048,512]{1,0:T(8,128)(2,1)}, f32[1,512]{1,0:T(1,128)}) custom-call(s32[4]{0:T(128)} %iota.8.pos_ref, bf16[2048,1024]{1,0:T(8,128)(2,1)} %copy-done.3, bf16[512,1152]{1,0:T(8,128)(2,1)} %copy-done.4, f32[2048,1]{1,0:T(8,128)} %copy.25.treated_ref, f32[2048,1]{1,0:T(8,128)} %copy.26.counter_ref), custom_call_target="tpu_custom_call" | custom-call | flops 2147483648 | bytes 4194304 | tf_op jit(solution)/shard_map/pallas_call | solution.py:67
  122.8 27.5 %shard_map.106.x_in_ref = f32[512,1664]{1,0:T(8,128)} custom-call(s32[1]{0:T(128)} %bitcast.5.shift_ref, bf16[2048,512]{1,0:T(8,128)(2,1)} %get-tuple-element.24.feat_panel_ref.refs_11_, bf16[2048,512]{1,0:T(8,128)(2,1)} %get-tuple-element.25.feat_ref.refs_10_, f32[1,512]{1,0:T(1,128)} %get-tuple-element.26.moment_panel_ref), custom_call_target="tpu_custom_call" | custom-call | flops 20000000000 | bytes 8000000 | tf_op jit(solution)/shard_map/pallas_call | solution.py:196
  150.4 0.1 collective-permute-start.5
  150.4 0.5 collective-permute-start.6
  150.9 0.1 collective-permute-start.7
  151.0 22.3 %shard_map.107 = (bf16[512,512]{1,0:T(8,128)(2,1)}, bf16[512,512]{1,0:T(8,128)(2,1)}, bf16[512,512]{1,0:T(8,128)(2,1)}, bf16[512,512]{1,0:T(8,128)(2,1)}, f32[1,512]{1,0:T(1,128)}) custom-call(f32[512,1664]{1,0:T(8,128)} %shard_map.106.x_in_ref, f32[1,512]{1,0:T(1,128)} %get-tuple-element.31.moment_ref), custom_call_target="tpu_custom_call" | custom-call | flops 20000000000 | bytes 8000000 | tf_op jit(solution)/shard_map/pallas_call | solution.py:211
  173.3 0.6 iota.7.pos_ref
  173.9 0.4 copy-done.8
  174.3 0.4 copy-done.9
  174.7 0.4 copy-done.10
  175.0 0.4 copy-done.11
  175.4 67.7 %shard_map.108 = (f32[4096,512]{1,0:T(8,128)}, f32[4096,512]{1,0:T(8,128)}) custom-call(s32[8]{0:T(128)} %broadcast_xor_fusion.order_ref, s32[3]{0:T(128)} %pad_add_fusion.place_ref, s32[4]{0:T(128)} %iota.7.pos_ref, bf16[512,1152]{1,0:T(8,128)(2,1)} %copy-done.2, bf16[512,1152]{1,0:T(8,128)(2,1)} %collective-permute-done.1.refs_1_, ...), custom_call_target="tpu_custom_call" | custom-call | flops 47244640256 | bytes 30000000 | tf_op jit(solution)/shard_map/pallas_call | solution.py:308
  (39 shorter events, 0.2 us)
Async XLA Ops:
  3.8 2.0 copy-start.1
  4.1 67.8 %copy-start = (bf16[512,1152]{1,0:T(8,128)(2,1)}, bf16[512,1152]{1,0:T(8,128)(2,1)S(1)}, u32[]{:S(2)}) copy-start(bf16[512,1152]{1,0:T(8,128)(2,1)S(1)} %get-tuple-element.39.freq_ref) | copy-start | bytes 3538948
  5.8 83.5 %copy-start.6 = (s32[1024]{0:T(1024)S(1)}, s32[1024]{0:T(1024)}, u32[]{:S(2)}) copy-start(s32[1024]{0:T(1024)} %param.12) | copy-start | bytes 12292
  5.8 83.5 %copy-start.7 = (s32[1024]{0:T(1024)S(1)}, s32[1024]{0:T(1024)}, u32[]{:S(2)}) copy-start(s32[1024]{0:T(1024)} %param.13) | copy-start | bytes 12292
  5.8 87.7 %copy-start.12 = (s32[8]{0:T(128)S(1)}, s32[8]{0:T(128)}, u32[]{:S(2)}) copy-start(s32[8]{0:T(128)} %constant.52.clone) | copy-start | bytes 100
  71.9 2.0 copy-start.3
  73.9 1.0 copy-start.4
  74.9 35.4 %copy-start.2 = (bf16[512,1152]{1,0:T(8,128)(2,1)}, bf16[512,1152]{1,0:T(8,128)(2,1)S(1)}, u32[]{:S(2)}) copy-start(bf16[512,1152]{1,0:T(8,128)(2,1)S(1)} %get-tuple-element.21.refs_0_) | copy-start | bytes 3538948
  74.9 98.4 %collective-permute-start.4 = (bf16[512,1152]{1,0:T(8,128)(2,1)S(1)}, bf16[512,1152]{1,0:T(8,128)(2,1)S(1)}, u32[]{:S(2)}, u32[]{:S(2)}) collective-permute-start(bf16[512,1152]{1,0:T(8,128)(2,1)S(1)} %get-tuple-element.21.refs_0_), channel_id=1, source_target_pairs={{0,1},{1,0},{2,3},{3,2},{4,5},{5,4},{6,7},{7,6},{8,9},{9,8},{10,11... | collective-permute-start | bytes 3538952 | tf_op jit(solution)/shard_map/ppermute | solution.py:458
  75.1 75.3 %collective-permute-start.3 = (bf16[512,1152]{1,0:T(8,128)(2,1)S(1)}, bf16[512,1152]{1,0:T(8,128)(2,1)}, u32[]{:S(2)}, u32[]{:S(2)}) collective-permute-start(bf16[512,1152]{1,0:T(8,128)(2,1)S(1)} %get-tuple-element.21.refs_0_), channel_id=1, source_target_pairs={{0,6},{1,7},{2,4},{3,5},{4,2},{5,3},{6,0},{7,1},{8,14},{9,15},{10,... | collective-permute-start | bytes 3538952 | tf_op jit(solution)/shard_map/ppermute | solution.py:458
  87.8 62.5 %collective-permute-start.2 = (bf16[512,1152]{1,0:T(8,128)(2,1)S(1)}, bf16[512,1152]{1,0:T(8,128)(2,1)}, u32[]{:S(2)}, u32[]{:S(2)}) collective-permute-start(bf16[512,1152]{1,0:T(8,128)(2,1)S(1)} %get-tuple-element.21.refs_0_), channel_id=1, source_target_pairs={{0,2},{1,3},{2,0},{3,1},{4,6},{5,7},{6,4},{7,5},{8,10},{9,11},{10,... | collective-permute-start | bytes 3538952 | tf_op jit(solution)/shard_map/ppermute | solution.py:458
  89.3 61.0 %collective-permute-start.1 = (bf16[512,1152]{1,0:T(8,128)(2,1)S(1)}, bf16[512,1152]{1,0:T(8,128)(2,1)}, u32[]{:S(2)}, u32[]{:S(2)}) collective-permute-start(bf16[512,1152]{1,0:T(8,128)(2,1)S(1)} %get-tuple-element.21.refs_0_), channel_id=1, source_target_pairs={{0,4},{1,5},{2,6},{3,7},{4,0},{5,1},{6,2},{7,3},{8,12},{9,13},{10,... | collective-permute-start | bytes 3538952 | tf_op jit(solution)/shard_map/ppermute | solution.py:458
  89.4 5.7 %collective-permute-start = (f32[2,1024]{1,0:T(2,128)S(1)}, f32[2,1024]{1,0:T(2,128)S(1)}, u32[]{:S(2)}, u32[]{:S(2)}) collective-permute-start(f32[2,1024]{1,0:T(2,128)S(1)} %pad_maximum_fusion.1), channel_id=1, source_target_pairs={{0,16},{16,0},{1,17},{17,1},{2,18},{18,2},{3,19},{19,3},{4,20},{20... | collective-permute-start | bytes 24584 | tf_op jit(solution)/shard_map/ppermute | solution.py:484
  95.2 15.2 %copy-start.5 = (f32[1,2048]{1,0:T(1,128)}, f32[1,2048]{1,0:T(1,128)S(1)}, u32[]{:S(2)}) copy-start(f32[1,2048]{1,0:T(1,128)S(1)} %get-tuple-element.42.refs_9_) | copy-start | bytes 24580
  150.4 22.9 %collective-permute-start.5 = (bf16[512,1152]{1,0:T(8,128)(2,1)}, bf16[512,1152]{1,0:T(8,128)(2,1)S(1)}, u32[]{:S(2)}, u32[]{:S(2)}) collective-permute-start(bf16[512,1152]{1,0:T(8,128)(2,1)} %collective-permute-done.1.refs_1_), channel_id=1, source_target_pairs={{0,1},{1,0},{2,3},{3,2},{4,5},{5,4},{6,7},{7,6},{8,9},{9,8},{10,11... | collective-permute-start | bytes 3538952 | tf_op jit(solution)/shard_map/ppermute | solution.py:458
  150.4 22.9 %collective-permute-start.6 = (bf16[512,1152]{1,0:T(8,128)(2,1)}, bf16[512,1152]{1,0:T(8,128)(2,1)S(1)}, u32[]{:S(2)}, u32[]{:S(2)}) collective-permute-start(bf16[512,1152]{1,0:T(8,128)(2,1)} %collective-permute-done.2.refs_2_), channel_id=1, source_target_pairs={{0,1},{1,0},{2,3},{3,2},{4,5},{5,4},{6,7},{7,6},{8,9},{9,8},{10,11... | collective-permute-start | bytes 3538952 | tf_op jit(solution)/shard_map/ppermute | solution.py:458
  150.9 22.4 %collective-permute-start.7 = (bf16[512,1152]{1,0:T(8,128)(2,1)}, bf16[512,1152]{1,0:T(8,128)(2,1)S(1)}, u32[]{:S(2)}, u32[]{:S(2)}) collective-permute-start(bf16[512,1152]{1,0:T(8,128)(2,1)} %collective-permute-done.3.refs_3_), channel_id=1, source_target_pairs={{0,1},{1,0},{2,3},{3,2},{4,5},{5,4},{6,7},{7,6},{8,9},{9,8},{10,11... | collective-permute-start | bytes 3538952 | tf_op jit(solution)/shard_map/ppermute | solution.py:458
  173.3 1.0 copy-start.8
  173.3 1.4 copy-start.9
  173.3 1.7 copy-start.10
  173.3 2.1 copy-start.11
